TPU v7x, 128 devices: a whole 4x4x4 slice. The times are simulated.
128 devices in a mesh: ctx: 32 (over z_hi, x, y), tp: 4 (over z_lo, core).
Axes of the slice: x: 4, y: 4, z: 4 (z_hi: 2, z_lo: 2; z = z_hi * 2 + z_lo), core: 2. Of those that a mesh axis runs over, the one named last changes fastest.
Arguments:
- tokens: bfloat16 [8192, 4096], P('ctx', 'tp'), may hold values from -6 to 6
- proj_weight: bfloat16 [3, 4096, 4096], P(None, None, 'tp'), may hold values from -0.09375 to 0.09375
- short_taps: float32 [3, 3, 4096], P(None, None, 'tp'), may hold values from -3 to 3
- residues: float32 [4096, 16], P('tp'), may hold values from -0.12 to 0.12
- rates: float32 [4096, 16], P('tp'), may hold values from 3.6621095e-05 to 0.05
- skip: float32 [4096], P('tp'), may hold values from -4 to 4
Outputs:
- gated: bfloat16 [8192, 4096], P('ctx', 'tp')
All inputs are finite; a program needn't handle non-finite values.
Results may differ from a plain program's by a relative error of at most 0.0085.
Values may be sent and summed in bfloat16 or wider, within the bound.
A program may use at most 128 MiB of HBM per device.

v0:
```python
import jax
import jax.numpy as jnp
from jax import lax
from jax.sharding import PartitionSpec as P

SUB = 32


def passed_along(block, axis, distance):
    devices = range(lax.axis_size(axis))
    route = [(i - distance, i) for i in devices if i - distance in devices]
    return lax.ppermute(block, axis, route)


def long_conv(source_f, residues, rates, sub, init):
    length, width = source_f.shape
    res_t = residues.T
    rate_t = rates.T
    lags = jnp.arange(sub).astype(jnp.float32)
    filt = jnp.sum(res_t[None] * jnp.exp(-rate_t[None] * lags[:, None, None]), axis=1)
    rows = jnp.arange(sub)
    lag = rows[:, None] - rows[None, :]
    band = jnp.where((lag >= 0)[:, :, None], filt[jnp.clip(lag, 0, sub - 1)], 0.0)
    back = jnp.exp(-rate_t[None] * (sub - 1.0 - lags)[:, None, None])
    ahead = res_t[None] * jnp.exp(-rate_t[None] * (lags + 1.0)[:, None, None])
    factor = jnp.exp(-rate_t * float(sub))

    def step(state, src):
        out = jnp.sum(band * src[None], axis=1) + jnp.sum(ahead * state[None], axis=1)
        state = factor * state + jnp.sum(back * src[:, None, :], axis=0)
        return (state, out)

    final, outs = lax.scan(step, init, source_f.reshape(length // sub, sub, width))
    return (final, outs.reshape(length, width))


def shards(tokens, proj_weight, short_taps, residues, rates, skip):
    tok_rows = tokens.shape[0]
    width = proj_weight.shape[2]
    order = residues.shape[1]
    taps = short_taps.shape[1]
    rim = taps - 1
    own_start = lax.axis_index("ctx") * tok_rows
    rate_t = rates.T
    projected = jnp.einsum(
        "tf,jfc->jtc",
        lax.all_gather(tokens, "tp", axis=1, tiled=True),
        proj_weight,
        preferred_element_type=jnp.float32,
    ).astype(jnp.bfloat16)
    before = passed_along(projected[:, tok_rows - rim :], "ctx", 1)
    padded = jnp.concatenate([before, projected], 1)
    padded = padded.astype(jnp.float32)
    mixed = sum(
        (
            short_taps[:, m][:, None, :] * padded[:, rim - m : rim - m + tok_rows]
            for m in range(taps)
        )
    )
    source = (mixed[1] * mixed[2]).astype(jnp.bfloat16)
    source_f = source.astype(jnp.float32)
    zero_state = jnp.zeros((order, width), jnp.float32)
    local_state, conv = long_conv(source_f, residues, rates, SUB, zero_state)
    piece = lax.all_gather(source, "ctx", axis=0, tiled=True)
    count = piece.shape[0]
    block_rows = 512
    turns = count // block_rows

    def add_rows(index, acc):
        first = index * block_rows
        rows_f = lax.dynamic_slice_in_dim(piece, first, block_rows, 0).astype(jnp.float32)
        position = first + jnp.arange(block_rows)
        valid = position < own_start
        expo = jnp.where(valid, own_start - 1 - position, 0).astype(jnp.float32)
        weights = jnp.where(valid[:, None, None], jnp.exp(-rate_t[None] * expo[:, None, None]), 0.0)
        return acc + jnp.sum(weights * rows_f[:, None, :], axis=0)

    def work(acc):
        return lax.fori_loop(0, turns, add_rows, acc)

    prior = lax.cond(jnp.int32(0) < own_start, work, lambda acc: acc, zero_state)
    rows_f = jnp.arange(tok_rows).astype(jnp.float32)
    ahead_full = residues.T[None] * jnp.exp(-rate_t[None] * (rows_f + 1.0)[:, None, None])
    conv = conv + jnp.sum(ahead_full * prior[None], axis=1)
    return (mixed[0] * (conv + skip[None, :] * source_f)).astype(jnp.bfloat16)


def solution(mesh):
    return jax.shard_map(
        shards,
        mesh=mesh,
        in_specs=(
            P("ctx", "tp"),
            P(None, None, "tp"),
            P(None, None, "tp"),
            P("tp", None),
            P("tp", None),
            P("tp"),
        ),
        out_specs=P("ctx", "tp"),
        check_vma=False,
    )
```

profile of v0, /device:TPU:96, one launch (start us, length us, event | category | flops | bytes accessed | tf_op | source)
XLA Modules:
  0.0 414.1 jit_solution(14733468278053826699)
XLA Ops:
  8.3 30.3 %all-gather.4.cloned.1.call-done = bf16[256,4096]{1,0:T(8,128)(2,1)} async-done(((bf16[256,1024]{1,0:T(8,128)(2,1)}), bf16[256,4096]{1,0:T(8,128)(2,1)}) %all-gather.4.cloned.1.call-update) | async-done | bytes 2097168 | tf_op jit(solution)/shard_map/all_gather | solution.py:47
  38.6 12.2 %fusion.14 = bf16[3,256,1024]{2,1,0:T(8,128)(2,1)S(1)} fusion(bf16[3,4096,1024]{2,1,0:T(8,128)(2,1)} %param.13, bf16[256,4096]{1,0:T(8,128)(2,1)} %all-gather.4.cloned.1.call-done), kind=kOutput, calls=%fused_computation.31 | convolution fusion | flops 6443237376 | bytes 28835840 | tf_op jit(solution)/shard_map/tf,jfc->jtc/dot_general | solution.py:45
  54.2 7.9 %collective-permute-done = bf16[3,2,1024]{2,1,0:T(2,128)(2,1)S(1)} collective-permute-done((bf16[3,2,1024]{2,1,0:T(2,128)(2,1)S(1)}, bf16[3,2,1024]{2,1,0:T(2,128)(2,1)S(1)}, u32[]{:S(2)}, u32[]{:S(2)}) %collective-permute-start) | collective-permute-done | bytes 12320 | tf_op jit(solution)/shard_map/ppermute | solution.py:12
  77.5 45.5 %while.31 = (s32[]{:T(128)}, f32[16,1024]{1,0:T(8,128)S(1)}, f32[8,32,1024]{2,1,0:T(8,128)}, f32[16,1024]{1,0:T(8,128)S(1)}, f32[8,32,1024]{2,1,0:T(8,128)}, /*i...) while((s32[]{:T(128)}, f32[16,1024]{1,0:T(8,128)S(1)}, ...), condition=%wide.region_5.6_spmd.clone.clone.clone, body=%wide.region_1.5_spmd.clone.clone.clone.sunk | while | flops 5783555 | bytes 6029712 | solution.py:33
  123.1 93.1 %all-gather.6.cloned.1.call-done = bf16[1,8192,1024]{2,1,0:T(8,128)(2,1)} async-done(((bf16[1,256,1024]{2,1,0:T(8,128)(2,1)}), bf16[1,8192,1024]{2,1,0:T(8,128)(2,1)}) %all-gather.6.cloned.1.call-update) | async-done | bytes 16777232 | tf_op jit(solution)/shard_map/all_gather | solution.py:64
  216.2 183.3 %conditional.1 = (f32[16,1024]{1,0:T(8,128)}) conditional(s32[]{:T(128)} %convert_element_type.86, () %tuple.37, (f32[16,1024]{1,0:T(8,128)S(1)}, s32[]{:T(128)}, bf16[8192,1024]{1,0:T(8,128)(2,1)}) %tuple.90), branch_computations={%region_6.7_spmd, %region_7.11_spmd} | conditional | flops 34115076 | bytes 5707049 | solution.py:81
  216.2 183.3 %while.30 = (s32[]{:T(128)}, f32[16,1024]{1,0:T(8,128)}, s32[]{:T(128)}, f32[1,16,1024]{2,1,0:T(8,128)S(1)}, s32[]{:T(128)}, /*index=5*/bf16[8192,1024]{1,0:T(8,...) while((s32[]{:T(128)}, f32[16,1024]{1,0:T(8,128)}, s32[]{:T(128)}, ...), condition=%wide.region_10.10_spmd.clone, body=%wide.region_8.9_spmd.clone.sunk | while | flops 34098692 | bytes 5575869 | solution.py:79
  217.7 8.5 %multiply_reduce_fusion.7 = f32[16,1024]{1,0:T(8,128)S(1)} fusion(f32[512,1024]{1,0:T(8,128)S(1)} %dynamic-slice_convert_fusion.2, f32[512]{0:T(512)S(1)} %select_convert_fusion.2, f32[16,1024]{1,0:T(8,128)S(1)} %bitcast.62, pred[512]{0:T(512)(128)(4,1)S(1)} %fusion.26), kind=kLoop, calls=%fused_computation.3.clone.1 | loop fusion | flops 33538048 | bytes 2230784 | tf_op jit(solution)/shard_map/cond/branch_1_fun/while/body/eval_jaxpr/reduce_sum | solution.py:76
  228.4 8.5 %multiply_reduce_fusion.7 = f32[16,1024]{1,0:T(8,128)S(1)} fusion(f32[512,1024]{1,0:T(8,128)S(1)} %dynamic-slice_convert_fusion.2, f32[512]{0:T(512)S(1)} %select_convert_fusion.2, f32[16,1024]{1,0:T(8,128)S(1)} %bitcast.62, pred[512]{0:T(512)(128)(4,1)S(1)} %fusion.26), kind=kLoop, calls=%fused_computation.3.clone.1 | loop fusion | flops 33538048 | bytes 2230784 | tf_op jit(solution)/shard_map/cond/branch_1_fun/while/body/eval_jaxpr/reduce_sum | solution.py:76
  239.9 8.5 %multiply_reduce_fusion.7 = f32[16,1024]{1,0:T(8,128)S(1)} fusion(f32[512,1024]{1,0:T(8,128)S(1)} %dynamic-slice_convert_fusion.2, f32[512]{0:T(512)S(1)} %select_convert_fusion.2, f32[16,1024]{1,0:T(8,128)S(1)} %bitcast.62, pred[512]{0:T(512)(128)(4,1)S(1)} %fusion.26), kind=kLoop, calls=%fused_computation.3.clone.1 | loop fusion | flops 33538048 | bytes 2230784 | tf_op jit(solution)/shard_map/cond/branch_1_fun/while/body/eval_jaxpr/reduce_sum | solution.py:76
  251.4 8.5 %multiply_reduce_fusion.7 = f32[16,1024]{1,0:T(8,128)S(1)} fusion(f32[512,1024]{1,0:T(8,128)S(1)} %dynamic-slice_convert_fusion.2, f32[512]{0:T(512)S(1)} %select_convert_fusion.2, f32[16,1024]{1,0:T(8,128)S(1)} %bitcast.62, pred[512]{0:T(512)(128)(4,1)S(1)} %fusion.26), kind=kLoop, calls=%fused_computation.3.clone.1 | loop fusion | flops 33538048 | bytes 2230784 | tf_op jit(solution)/shard_map/cond/branch_1_fun/while/body/eval_jaxpr/reduce_sum | solution.py:76
  262.9 8.5 %multiply_reduce_fusion.7 = f32[16,1024]{1,0:T(8,128)S(1)} fusion(f32[512,1024]{1,0:T(8,128)S(1)} %dynamic-slice_convert_fusion.2, f32[512]{0:T(512)S(1)} %select_convert_fusion.2, f32[16,1024]{1,0:T(8,128)S(1)} %bitcast.62, pred[512]{0:T(512)(128)(4,1)S(1)} %fusion.26), kind=kLoop, calls=%fused_computation.3.clone.1 | loop fusion | flops 33538048 | bytes 2230784 | tf_op jit(solution)/shard_map/cond/branch_1_fun/while/body/eval_jaxpr/reduce_sum | solution.py:76
  274.4 8.5 %multiply_reduce_fusion.7 = f32[16,1024]{1,0:T(8,128)S(1)} fusion(f32[512,1024]{1,0:T(8,128)S(1)} %dynamic-slice_convert_fusion.2, f32[512]{0:T(512)S(1)} %select_convert_fusion.2, f32[16,1024]{1,0:T(8,128)S(1)} %bitcast.62, pred[512]{0:T(512)(128)(4,1)S(1)} %fusion.26), kind=kLoop, calls=%fused_computation.3.clone.1 | loop fusion | flops 33538048 | bytes 2230784 | tf_op jit(solution)/shard_map/cond/branch_1_fun/while/body/eval_jaxpr/reduce_sum | solution.py:76
  285.9 8.5 %multiply_reduce_fusion.7 = f32[16,1024]{1,0:T(8,128)S(1)} fusion(f32[512,1024]{1,0:T(8,128)S(1)} %dynamic-slice_convert_fusion.2, f32[512]{0:T(512)S(1)} %select_convert_fusion.2, f32[16,1024]{1,0:T(8,128)S(1)} %bitcast.62, pred[512]{0:T(512)(128)(4,1)S(1)} %fusion.26), kind=kLoop, calls=%fused_computation.3.clone.1 | loop fusion | flops 33538048 | bytes 2230784 | tf_op jit(solution)/shard_map/cond/branch_1_fun/while/body/eval_jaxpr/reduce_sum | solution.py:76
  297.4 8.5 %multiply_reduce_fusion.7 = f32[16,1024]{1,0:T(8,128)S(1)} fusion(f32[512,1024]{1,0:T(8,128)S(1)} %dynamic-slice_convert_fusion.2, f32[512]{0:T(512)S(1)} %select_convert_fusion.2, f32[16,1024]{1,0:T(8,128)S(1)} %bitcast.62, pred[512]{0:T(512)(128)(4,1)S(1)} %fusion.26), kind=kLoop, calls=%fused_computation.3.clone.1 | loop fusion | flops 33538048 | bytes 2230784 | tf_op jit(solution)/shard_map/cond/branch_1_fun/while/body/eval_jaxpr/reduce_sum | solution.py:76
  308.9 8.5 %multiply_reduce_fusion.7 = f32[16,1024]{1,0:T(8,128)S(1)} fusion(f32[512,1024]{1,0:T(8,128)S(1)} %dynamic-slice_convert_fusion.2, f32[512]{0:T(512)S(1)} %select_convert_fusion.2, f32[16,1024]{1,0:T(8,128)S(1)} %bitcast.62, pred[512]{0:T(512)(128)(4,1)S(1)} %fusion.26), kind=kLoop, calls=%fused_computation.3.clone.1 | loop fusion | flops 33538048 | bytes 2230784 | tf_op jit(solution)/shard_map/cond/branch_1_fun/while/body/eval_jaxpr/reduce_sum | solution.py:76
  320.4 8.5 %multiply_reduce_fusion.7 = f32[16,1024]{1,0:T(8,128)S(1)} fusion(f32[512,1024]{1,0:T(8,128)S(1)} %dynamic-slice_convert_fusion.2, f32[512]{0:T(512)S(1)} %select_convert_fusion.2, f32[16,1024]{1,0:T(8,128)S(1)} %bitcast.62, pred[512]{0:T(512)(128)(4,1)S(1)} %fusion.26), kind=kLoop, calls=%fused_computation.3.clone.1 | loop fusion | flops 33538048 | bytes 2230784 | tf_op jit(solution)/shard_map/cond/branch_1_fun/while/body/eval_jaxpr/reduce_sum | solution.py:76
  331.9 8.5 %multiply_reduce_fusion.7 = f32[16,1024]{1,0:T(8,128)S(1)} fusion(f32[512,1024]{1,0:T(8,128)S(1)} %dynamic-slice_convert_fusion.2, f32[512]{0:T(512)S(1)} %select_convert_fusion.2, f32[16,1024]{1,0:T(8,128)S(1)} %bitcast.62, pred[512]{0:T(512)(128)(4,1)S(1)} %fusion.26), kind=kLoop, calls=%fused_computation.3.clone.1 | loop fusion | flops 33538048 | bytes 2230784 | tf_op jit(solution)/shard_map/cond/branch_1_fun/while/body/eval_jaxpr/reduce_sum | solution.py:76
  343.4 8.5 %multiply_reduce_fusion.7 = f32[16,1024]{1,0:T(8,128)S(1)} fusion(f32[512,1024]{1,0:T(8,128)S(1)} %dynamic-slice_convert_fusion.2, f32[512]{0:T(512)S(1)} %select_convert_fusion.2, f32[16,1024]{1,0:T(8,128)S(1)} %bitcast.62, pred[512]{0:T(512)(128)(4,1)S(1)} %fusion.26), kind=kLoop, calls=%fused_computation.3.clone.1 | loop fusion | flops 33538048 | bytes 2230784 | tf_op jit(solution)/shard_map/cond/branch_1_fun/while/body/eval_jaxpr/reduce_sum | solution.py:76
  355.0 8.5 %multiply_reduce_fusion.7 = f32[16,1024]{1,0:T(8,128)S(1)} fusion(f32[512,1024]{1,0:T(8,128)S(1)} %dynamic-slice_convert_fusion.2, f32[512]{0:T(512)S(1)} %select_convert_fusion.2, f32[16,1024]{1,0:T(8,128)S(1)} %bitcast.62, pred[512]{0:T(512)(128)(4,1)S(1)} %fusion.26), kind=kLoop, calls=%fused_computation.3.clone.1 | loop fusion | flops 33538048 | bytes 2230784 | tf_op jit(solution)/shard_map/cond/branch_1_fun/while/body/eval_jaxpr/reduce_sum | solution.py:76
  366.5 8.5 %multiply_reduce_fusion.7 = f32[16,1024]{1,0:T(8,128)S(1)} fusion(f32[512,1024]{1,0:T(8,128)S(1)} %dynamic-slice_convert_fusion.2, f32[512]{0:T(512)S(1)} %select_convert_fusion.2, f32[16,1024]{1,0:T(8,128)S(1)} %bitcast.62, pred[512]{0:T(512)(128)(4,1)S(1)} %fusion.26), kind=kLoop, calls=%fused_computation.3.clone.1 | loop fusion | flops 33538048 | bytes 2230784 | tf_op jit(solution)/shard_map/cond/branch_1_fun/while/body/eval_jaxpr/reduce_sum | solution.py:76
  378.0 8.5 %multiply_reduce_fusion.7 = f32[16,1024]{1,0:T(8,128)S(1)} fusion(f32[512,1024]{1,0:T(8,128)S(1)} %dynamic-slice_convert_fusion.2, f32[512]{0:T(512)S(1)} %select_convert_fusion.2, f32[16,1024]{1,0:T(8,128)S(1)} %bitcast.62, pred[512]{0:T(512)(128)(4,1)S(1)} %fusion.26), kind=kLoop, calls=%fused_computation.3.clone.1 | loop fusion | flops 33538048 | bytes 2230784 | tf_op jit(solution)/shard_map/cond/branch_1_fun/while/body/eval_jaxpr/reduce_sum | solution.py:76
  389.5 8.5 %multiply_reduce_fusion.7 = f32[16,1024]{1,0:T(8,128)S(1)} fusion(f32[512,1024]{1,0:T(8,128)S(1)} %dynamic-slice_convert_fusion.2, f32[512]{0:T(512)S(1)} %select_convert_fusion.2, f32[16,1024]{1,0:T(8,128)S(1)} %bitcast.62, pred[512]{0:T(512)(128)(4,1)S(1)} %fusion.26), kind=kLoop, calls=%fused_computation.3.clone.1 | loop fusion | flops 33538048 | bytes 2230784 | tf_op jit(solution)/shard_map/cond/branch_1_fun/while/body/eval_jaxpr/reduce_sum | solution.py:76
  399.5 6.4 %multiply_reduce_fusion.2 = f32[256,1024]{1,0:T(8,128)S(1)} fusion(f32[16,1024]{1,0:T(8,128)} %get-tuple-element.523, f32[256]{0:T(256)S(1)} %convert_add_fusion, f32[16,1024]{1,0:T(8,128)S(1)} %get-tuple-element.531, f32[16,1024]{1,0:T(8,128)S(1)} %get-tuple-element.535), kind=kLoop, calls=%fused_computation.19 | loop fusion | flops 16515072 | bytes 1246208 | tf_op jit(solution)/shard_map/reduce_sum | solution.py:84
  (151 shorter events, 114.0 us)
Async XLA Ops:
  6.5 32.0 %all-gather.4.cloned.1.call-start = ((), (), s32[]{:S(2)}) async-start(), calls=%async_computation | async-start | bytes 2621440 | tf_op jit(solution)/shard_map/all_gather | solution.py:47
  7.3 208.9 %all-gather.6.cloned.1.call-start = ((), (), s32[]{:S(2)}) async-start(), calls=%async_computation.1 | async-start | bytes 17301504 | tf_op jit(solution)/shard_map/all_gather | solution.py:64
  50.8 11.3 %collective-permute-start = (bf16[3,2,1024]{2,1,0:T(2,128)(2,1)S(1)}, bf16[3,2,1024]{2,1,0:T(2,128)(2,1)S(1)}, u32[]{:S(2)}, u32[]{:S(2)}) collective-permute-start(bf16[3,2,1024]{2,1,0:T(2,128)(2,1)S(1)} %slice.42), channel_id=1, source_target_pairs={{0,4},{4,8},{8,12},{12,16},{16,20},{20,24},{24,28},{28,32},{32,36}... | collective-permute-start | bytes 36872 | tf_op jit(solution)/shard_map/ppermute | solution.py:12
  63.5 1.1 copy-start.2
  71.6 4.9 %copy-start = (bf16[1,256,1024]{2,1,0:T(8,128)(2,1)S(1)}, bf16[1,256,1024]{2,1,0:T(8,128)(2,1)}, u32[]{:S(2)}) copy-start(bf16[1,256,1024]{2,1,0:T(8,128)(2,1)} %fusion.17) | copy-start | bytes 1572868
  71.6 6.0 %copy-start.4 = (f32[1024,16]{0,1:T(8,128)S(1)}, f32[1024,16]{0,1:T(8,128)}, u32[]{:S(2)}) copy-start(f32[1024,16]{0,1:T(8,128)} %param.15) | copy-start | bytes 196612
  399.5 6.4 %copy-start.1 = (f32[8,32,1024]{2,1,0:T(8,128)S(1)}, f32[8,32,1024]{2,1,0:T(8,128)}, u32[]{:S(2)}) copy-start(f32[8,32,1024]{2,1,0:T(8,128)} %get-tuple-element.194) | copy-start | bytes 3145732
  399.5 6.4 %copy-start.3 = (f32[1024]{0:T(1024)S(1)}, f32[1024]{0:T(1024)}, u32[]{:S(2)}) copy-start(f32[1024]{0:T(1024)} %param.17) | copy-start | bytes 12292
Sparse Core Ops, SparseCore 0:
  9.0 29.4 all-gather.3
  64.6 151.5 all-gather.5
where the time goes:
time: 419 us; the launch traced here: 414 us
  other arithmetic  238 us (57%)
  waiting for transfers between devices  132 us (32%)
  local copies, waits for them, and re-layouts  13.9 us (3%)
  between operations  13.6 us (3%)
  matrix products  12.2 us (3%)
    reduce_sum x16, other arithmetic, add_rows(): return acc + jnp.sum(weights * rows_f[:, None, :], axis=0)  136 us
    all_gather x1, waiting for transfers between devices, shards(): piece = lax.all_gather(source, 'ctx', axis=0, tiled=True)  93.1 us
    all_gather x1, waiting for transfers between devices, shards(): lax.all_gather(tokens, 'tp', axis=1, tiled=True)  30.3 us
    convert_element_type x16, other arithmetic, add_rows(): lax.dynamic_slice_in_dim(piece, first, block_rows, 0).astype(jnp.float32)  23.5 us
    reduce_sum x8, other arithmetic, step(): jnp.sum(band * src[None], axis=1) + jnp.sum(ahead * state[None], axis=1)  23.4 us
    add x16, other arithmetic, add_rows(): return acc + jnp.sum(weights * rows_f[:, None, :], axis=0)  23 us
    dot_general x1, matrix products, shards(): jnp.einsum('tf,jfc->jtc', lax.all_gather(tokens, 'tp', axis=1, tiled=True...  12.2 us
    reduce_sum x8, other arithmetic, step(): jnp.sum(ahead * state[None], axis=1)  8.87 us
  transfers between devices with their start and end apart: 3, of which 3 were waited for; matrix products, arithmetic and copies ran while one was open for 14% of the time, Pallas kernels for 0%

commit v1 on v0

v1 whole, which is shorter than its diff:
```python
import jax
import jax.numpy as jnp
from jax import lax
from jax.experimental import pallas as pl
from jax.experimental.pallas import tpu as pltpu
from jax.sharding import PartitionSpec as P

MESH = pl.DeviceIdType.MESH
F32, BF16 = jnp.float32, jnp.bfloat16

ROWS = 256
HALO = 16
M = HALO + ROWS
WIDTH = 1024
ORDER = 16
LANE, SUBL = 128, 8
TILE = 256
TILES = WIDTH // TILE
NY = 4
STEP = 16
CHUNKS = ((0, 256), (256, 256), (512, 256), (768, 128), (896, 128))


def kernel(
    tokens, weight, taps, residues, rates, skip, out,
    w, x, acc, proj, src, base, gate, power, fac, fac_step, res, tail, pack, rim_out, rim_in, rim,
    taps_v, taps_t, rates_v, res_v, skip_v, state, row_in, row_tot, grid_in, wpre, wtot,
    w_sem, tok_sem, par_sem, sib_s, sib_r, far_s, far_r, fwd_s, fwd_r,
    rim_s, rim_r, row_s, row_r, grid_s, grid_r,
):
    ctx, tp = lax.axis_index("ctx"), lax.axis_index("tp")
    n_ctx = lax.axis_size("ctx")
    n_rows = n_ctx // NY
    y, g = ctx % NY, ctx // NY

    def partner(s):
        return (tp + 1 - 2 * (tp % 2), (tp + 2) % 4, 3 - tp)[s - 1] if s else tp

    def w_copy(s, j):
        rows = pl.ds(pl.multiple_of(partner(s) * WIDTH, WIDTH), WIDTH)
        return pltpu.make_async_copy(weight.at[j, rows, :], w.at[s, j], w_sem.at[s, j])

    own_copy = pltpu.make_async_copy(tokens, x.at[0, pl.ds(HALO, ROWS), :], tok_sem.at[0])
    tail_copy = pltpu.make_async_copy(tokens.at[pl.ds(ROWS - 16, 16), :], rim, tok_sem.at[1])
    par_copies = [
        pltpu.make_async_copy(a, b, par_sem.at[i])
        for i, (a, b) in enumerate(
            ((taps, taps_v), (residues, res_v), (rates, rates_v), (skip, skip_v))
        )
    ]
    tail_copy.start()
    own_copy.start()
    for s in range(4):
        for j in range(3):
            w_copy(s, j).start()
        if s == 0:
            for c in par_copies:
                c.start()

    barrier = pltpu.get_barrier_semaphore()

    def greet(c, t):
        pl.semaphore_signal(barrier, inc=1, device_id={"ctx": c, "tp": t}, device_id_type=MESH)

    greet(ctx, partner(1))
    greet(ctx, partner(2))
    for d in range(1, NY):
        greet(ctx - y + (y + NY - d) % NY, tp)

    @pl.when(ctx > 0)
    def _():
        for s in range(4):
            greet(ctx - 1, partner(s))

    @pl.loop(0, g)
    def _(k):
        greet(k * NY + y, tp)

    heard = 2 + (NY - 1) + 4 * jnp.where(ctx < n_ctx - 1, 1, 0) + (n_rows - 1 - g)
    pl.semaphore_wait(barrier, heard)

    def sib_copy():
        return pltpu.make_async_remote_copy(
            tokens, x.at[1, pl.ds(HALO, ROWS), :], sib_s, sib_r,
            device_id={"ctx": ctx, "tp": partner(1)}, device_id_type=MESH)

    def far_copy(i):
        cols = pl.ds(*CHUNKS[i])
        return pltpu.make_async_remote_copy(
            tokens.at[:, cols], x.at[2, pl.ds(HALO, ROWS), cols], far_s.at[i], far_r.at[i],
            device_id={"ctx": ctx, "tp": partner(2)}, device_id_type=MESH)

    def fwd_copy(i):
        cols = pl.ds(*CHUNKS[i])
        return pltpu.make_async_remote_copy(
            x.at[2, pl.ds(HALO, ROWS), cols], x.at[3, pl.ds(HALO, ROWS), cols],
            fwd_s.at[i], fwd_r.at[i],
            device_id={"ctx": ctx, "tp": partner(1)}, device_id_type=MESH)

    def rim_copy(s):
        return pltpu.make_async_remote_copy(
            rim_out, rim_in.at[s], rim_s.at[s], rim_r.at[s],
            device_id={"ctx": ctx + 1, "tp": partner(s)}, device_id_type=MESH)

    for i in range(len(CHUNKS)):
        far_copy(i).start()
    sib_copy().start()

    tail_copy.wait()
    tail[...] = rim[...].astype(F32)
    for c in range(SUBL):
        pack[2 * c:2 * c + 2, :] = tail[14:16, c * LANE:(c + 1) * LANE]
    rim_out[...] = pack[...].astype(BF16)

    @pl.when(ctx < n_ctx - 1)
    def _():
        for s in range(4):
            rim_copy(s).start()

    for c in par_copies:
        c.wait()

    def by_position(ref, first, value):
        count = value.shape[0]
        for c in range(SUBL):
            ref[pl.ds(first + c, count, stride=SUBL), :] = value[:, c * LANE:(c + 1) * LANE]

    for j in range(3):
        by_position(taps_t, j * 3 * SUBL, taps_v[j])
    by_position(res, 0, res_v[...])
    by_position(fac, 0, rates_v[...])
    rate = fac[...]
    for d in range(NY):
        below = (y + NY - d) % NY
        wtot[d] = jnp.exp(-rate * (ROWS * (NY - 1 - below)).astype(F32))
        if d:
            wpre[d - 1] = jnp.exp(-rate * float(ROWS * (d - 1))) * jnp.where(d <= y, 1.0, 0.0)
    fac_step[0] = jnp.exp(-rate * float(ROWS * NY))
    fac_step[1] = jnp.exp(-rate * (ROWS * y).astype(F32))
    fac[...] = jnp.exp(-rate)

    @pl.loop(0, STEP)
    def _(b):
        power[b] = jnp.exp(-rate * (b + 1).astype(F32))

    tail[...] = jnp.zeros_like(tail)
    for s in range(4):
        @pl.when(ctx > 0)
        def _(s=s):
            rim_copy(s).wait_recv()
            pack[...] = rim_in[s].astype(F32)
            for c in range(SUBL):
                tail[14:16, c * LANE:(c + 1) * LANE] = pack[2 * c:2 * c + 2, :]

        x[s, 0:HALO, :] = tail[...].astype(BF16)

    def tile_of(q):
        return q // TILES, pl.ds(pl.multiple_of((q % TILES) * TILE, TILE), TILE)

    own_copy.wait()
    for j in range(3):
        w_copy(0, j).wait()

        @pl.loop(j * TILES, (j + 1) * TILES)
        def _(q):
            _, cols = tile_of(q)
            acc[q] = jnp.dot(x[0], w[0, j, :, cols], preferred_element_type=F32)

    sib_copy().wait_recv()
    for j in range(3):
        w_copy(1, j).wait()

        @pl.loop(j * TILES, (j + 1) * TILES)
        def _(q):
            _, cols = tile_of(q)
            acc[q] += jnp.dot(x[1], w[1, j, :, cols], preferred_element_type=F32)

    def far_dots(i, q):
        j, cols = tile_of(q)
        first, size = CHUNKS[i]
        k = slice(first, first + size)
        return (
            jnp.dot(x[2, :, k], w[2, j, k, cols], preferred_element_type=F32)
            + jnp.dot(x[3, :, k], w[3, j, k, cols], preferred_element_type=F32)
        )

    last = len(CHUNKS) - 1
    for i in range(last + 1):
        far_copy(i).wait_recv()
        fwd_copy(i).start()
        if i == 0:
            for s in (2, 3):
                for j in range(3):
                    w_copy(s, j).wait()
        if i:
            fwd_copy(i - 1).wait_recv()

            @pl.loop(0, 3 * TILES)
            def _(q, i=i):
                acc[q] += far_dots(i - 1, q)

    def finish(q):
        value = (acc[q] + far_dots(last, q)).astype(BF16).astype(F32)
        first = (q // TILES) * (M * SUBL) + (q % TILES) * (TILE // LANE)
        for c in range(TILE // LANE):
            proj[pl.ds(first + c, M, stride=SUBL), :] = value[:, c * LANE:(c + 1) * LANE]

    fwd_copy(last).wait_recv()

    @pl.loop(TILES, 3 * TILES)
    def _(q):
        finish(q)

    def row(j, t):
        first = (j * M + HALO + t) * SUBL
        return proj[pl.ds(pl.multiple_of(first, SUBL), SUBL), :]

    def at(t):
        return pl.ds(pl.multiple_of(t * SUBL, SUBL), SUBL)

    def tap(j, m):
        first = (j * 3 + m) * SUBL
        return taps_t[first:first + SUBL, :]

    shape = (ORDER, SUBL, LANE)

    def state_step(i, carry):
        s, k1, k2, v1, v2 = carry
        f = fac[...].reshape(shape)
        for u in range(8):
            t = i * 8 + u
            k0, v0 = row(1, t), row(2, t)
            key = tap(1, 0) * k0 + tap(1, 1) * k1 + tap(1, 2) * k2
            value = tap(2, 0) * v0 + tap(2, 1) * v1 + tap(2, 2) * v2
            own = (key * value).astype(BF16).astype(F32)
            src[at(t), :] = own
            s = f * s + own[None]
            k1, k2, v1, v2 = k0, k1, v0, v1
        return s, k1, k2, v1, v2

    zero = jnp.zeros(shape, F32)
    own_state = lax.fori_loop(
        0, ROWS // 8, state_step, (zero, row(1, -1), row(1, -2), row(2, -1), row(2, -2)))[0]
    flat = own_state.reshape(ORDER * SUBL, LANE)
    state[...] = flat.astype(BF16)
    row_tot[0] = flat * wtot[0]

    def row_copy(d):
        return pltpu.make_async_remote_copy(
            state, row_in.at[d - 1], row_s.at[d - 1], row_r.at[d - 1],
            device_id={"ctx": ctx - y + (y + d) % NY, "tp": tp}, device_id_type=MESH)

    for d in range(1, NY):
        row_copy(d).start()

    @pl.loop(0, TILES)
    def _(q):
        finish(q)

    def local_step(i, carry):
        s, g1, g2 = carry
        f, r = fac[...].reshape(shape), res[...].reshape(shape)
        for u in range(8):
            t = i * 8 + u
            own, g0 = src[at(t), :], row(0, t)
            s = f * s + own[None]
            base[at(t), :] = jnp.sum(r * s, axis=0) + skip_v[...] * own
            gate[at(t), :] = tap(0, 0) * g0 + tap(0, 1) * g1 + tap(0, 2) * g2
            g1, g2 = g0, g1
        return s, g1, g2

    half = ROWS // 16
    carry = lax.fori_loop(0, half, local_step, (zero, row(0, -1), row(0, -2)))

    prior, total = jnp.zeros((ORDER * SUBL, LANE), F32), row_tot[0]
    for d in range(1, NY):
        row_copy(d).wait_recv()
        got = row_in[d - 1].astype(F32)
        prior += wpre[d - 1] * got
        total += wtot[d] * got
    row_tot[0] = prior
    for d in range(1, NY):
        row_copy(d).wait_send()
    state[...] = total.astype(BF16)

    def grid_copy(d):
        return pltpu.make_async_remote_copy(
            state, grid_in.at[d - 1], grid_s.at[d - 1], grid_r.at[d - 1],
            device_id={"ctx": ctx + NY * d, "tp": tp}, device_id_type=MESH)

    @pl.loop(1, n_rows - g)
    def _(d):
        grid_copy(d).start()

    lax.fori_loop(half, 2 * half, local_step, carry)

    def add_row(k, total):
        d = g - k
        grid_copy(d).wait_recv()
        return fac_step[0] * total + grid_in[d - 1].astype(F32)

    ahead = lax.fori_loop(0, g, add_row, jnp.zeros((ORDER * SUBL, LANE), F32))
    ahead = row_tot[0] + fac_step[1] * ahead

    def last_step(a, u):
        for b in range(STEP):
            t = a * STEP + b
            conv = jnp.sum(u * power[b].reshape(shape), axis=0) + base[at(t), :]
            base[at(t), :] = gate[at(t), :] * conv
        return u * power[STEP - 1].reshape(shape)

    lax.fori_loop(0, ROWS // STEP, last_step, (res[...] * ahead).reshape(shape))
    for c in range(SUBL):
        out[:, c * LANE:(c + 1) * LANE] = base[pl.ds(c, ROWS, stride=SUBL), :].astype(BF16)

    sib_copy().wait_send()
    for i in range(last + 1):
        far_copy(i).wait_send()
        fwd_copy(i).wait_send()

    @pl.when(ctx < n_ctx - 1)
    def _():
        for s in range(4):
            rim_copy(s).wait_send()

    @pl.loop(1, n_rows - g)
    def _(d):
        grid_copy(d).wait_send()


def shards(tokens, proj_weight, short_taps, residues, rates, skip):
    hbm = pl.BlockSpec(memory_space=pltpu.HBM)
    n_rows = lax.axis_size("ctx") // NY
    chunks = len(CHUNKS)
    flat = (ORDER * SUBL, LANE)
    dma = pltpu.SemaphoreType.DMA
    return pl.pallas_call(
        kernel,
        out_shape=jax.ShapeDtypeStruct((ROWS, WIDTH), BF16),
        in_specs=[hbm] * 6,
        out_specs=pl.BlockSpec(memory_space=pltpu.VMEM),
        scratch_shapes=[
            pltpu.VMEM((4, 3, WIDTH, WIDTH), BF16),
            pltpu.VMEM((4, M, WIDTH), BF16),
            pltpu.VMEM((3 * TILES, M, TILE), F32),
            pltpu.VMEM((3 * M * SUBL, LANE), F32),
            pltpu.VMEM((ROWS * SUBL, LANE), F32),
            pltpu.VMEM((ROWS * SUBL, LANE), F32),
            pltpu.VMEM((ROWS * SUBL, LANE), F32),
            pltpu.VMEM((STEP, *flat), F32),
            pltpu.VMEM(flat, F32),
            pltpu.VMEM((2, *flat), F32),
            pltpu.VMEM(flat, F32),
            pltpu.VMEM((16, WIDTH), F32),
            pltpu.VMEM((16, LANE), F32),
            pltpu.VMEM((16, LANE), BF16),
            pltpu.VMEM((4, 16, LANE), BF16),
            pltpu.VMEM((16, WIDTH), BF16),
            pltpu.VMEM((3, 3, WIDTH), F32),
            pltpu.VMEM((9 * SUBL, LANE), F32),
            pltpu.VMEM((ORDER, WIDTH), F32),
            pltpu.VMEM((ORDER, WIDTH), F32),
            pltpu.VMEM((SUBL, LANE), F32),
            pltpu.VMEM(flat, BF16),
            pltpu.VMEM((NY - 1, *flat), BF16),
            pltpu.VMEM((1, *flat), F32),
            pltpu.VMEM((n_rows - 1, *flat), BF16),
            pltpu.VMEM((NY - 1, *flat), F32),
            pltpu.VMEM((NY, *flat), F32),
            dma((4, 3)),
            dma((2,)),
            dma((4,)),
            dma, dma,
            dma((chunks,)), dma((chunks,)),
            dma((chunks,)), dma((chunks,)),
            dma((4,)), dma((4,)),
            dma((NY - 1,)), dma((NY - 1,)),
            dma((n_rows - 1,)), dma((n_rows - 1,)),
        ],
        compiler_params=pltpu.CompilerParams(
            collective_id=0, has_side_effects=True, vmem_limit_bytes=56 * 2**20),
        name="hyena",
    )(tokens, proj_weight, short_taps, residues.T, rates.T, skip.reshape(SUBL, LANE))


def solution(mesh):
    return jax.shard_map(
        shards,
        mesh=mesh,
        in_specs=(
            P("ctx", "tp"),
            P(None, None, "tp"),
            P(None, None, "tp"),
            P("tp", None),
            P("tp", None),
            P("tp"),
        ),
        out_specs=P("ctx", "tp"),
        check_vma=False,
    )
```

time: 419 us -> 50.1 us (0.12)
  other arithmetic: 238 us -> 0 us
  waiting for transfers between devices: 132 us -> 0 us
  Pallas kernels: 0 us -> 47.4 us
  between operations: 13.6 us -> 0.01 us
  matrix products: 12.2 us -> 0 us
  local copies, waits for them, and re-layouts: 13.9 us -> 1.87 us
    reduce_sum x34 -> x0, other arithmetic: 176 us -> none  [the longest x16 136 us: add_rows(): return acc + jnp.sum(weights * rows_f[:, None, :], axis=0)]
    all_gather x2 -> x0, waiting for transfers between devices: 123 us -> none  [the longest x1 93.1 us: shards(): piece = lax.all_gather(source, 'ctx', axis=0, tiled=True)]
    pallas_call x0 -> x1, Pallas kernels: none -> 47.4 us  [shards(): pl.pallas_call(kernel, out_shape=jax.ShapeDtypeStruct((ROWS, WIDTH), BF16...]
    convert_element_type x37 -> x0, other arithmetic: 27.5 us -> none  [the longest x16 23.5 us: add_rows(): lax.dynamic_slice_in_dim(piece, first, block_rows, 0).astype(jnp.float32)]
    add x27 -> x0, other arithmetic: 24.2 us -> none  [the longest x16 23 us: add_rows(): return acc + jnp.sum(weights * rows_f[:, None, :], axis=0)]
    dot_general x1 -> x0, matrix products: 12.2 us -> none  [shards(): jnp.einsum('tf,jfc->jtc', lax.all_gather(tokens, 'tp', axis=1, tiled=True...]
    ppermute x1 -> x0, waiting for transfers between devices: 7.88 us -> none  [passed_along(): return lax.ppermute(block, axis, route)]
    mul x8 -> x0, local copies, waits for them, and re-layouts: 7.4 us -> none  [step(): state = factor * state + jnp.sum(back * src[:, None, :], axis=0)]
  transfers between devices with their start and end apart: 3 -> 0, of which waited for: 3 -> 0; matrix products, arithmetic and copies ran while one was open for 14% -> 0% of each run, Pallas kernels for 0% -> 0%
where the time goes in v1:
time: 50.1 us; the launch traced here: 49.2 us
  Pallas kernels  47.4 us (95%)
  local copies, waits for them, and re-layouts  1.87 us (4%)
    pallas_call x1, Pallas kernels, shards(): pl.pallas_call(kernel, out_shape=jax.ShapeDtypeStruct((ROWS, WIDTH), BF16...  47.4 us
    unnamed x1, local copies, waits for them, and re-layouts  1.87 us

profile of v1, /device:TPU:96, one launch (start us, length us, event | category | flops | bytes accessed | tf_op | source)
XLA Modules:
  0.0 49.2 jit_solution(207908333643667189)
XLA Ops:
  0.0 47.4 %hyena.1 = bf16[256,1024]{1,0:T(8,128)(2,1)} custom-call(bf16[256,1024]{1,0:T(8,128)(2,1)} %tokens.1, bf16[3,4096,1024]{2,1,0:T(8,128)(2,1)} %weight.1, f32[3,3,1024]{2,1,0:T(4,128)} %taps.1, f32[16,1024]{1,0:T(8,128)} %bitcast.3, f32[16,1024]{1,0:T(8,128)} %bitcast.4, f32[8,128]{1,0:T(8,128)} %bitcast.5), custom_call_target="tpu_custom_call" | custom-call | tf_op jit(solution)/shard_map/hyena/pallas_call | solution.py:337
  47.4 1.9 %copy.8 = bf16[256,1024]{1,0:T(8,128)(2,1)} copy(bf16[256,1024]{1,0:T(8,128)(2,1)} %hyena.1) | data formatting | bytes 1048576

commit v2 on v1

--- a/solution.py
+++ b/solution.py
@@ -24,9 +24,9 @@
 def kernel(
     tokens, weight, taps, residues, rates, skip, out,
     w, x, acc, proj, src, base, gate, power, fac, fac_step, res, tail, pack, rim_out, rim_in, rim,
-    taps_v, taps_t, rates_v, res_v, skip_v, state, row_in, row_tot, grid_in, wpre, wtot,
+    taps_v, taps_t, rates_v, res_v, skip_v, state, row_sum, row_in, row_tot, grid_in, wpre, wtot,
     w_sem, tok_sem, par_sem, sib_s, sib_r, far_s, far_r, fwd_s, fwd_r,
-    rim_s, rim_r, row_s, row_r, grid_s, grid_r,
+    rim_s, rim_r, row_s, row_r, grid_s, grid_r, rim_ok, row_ok, grid_ok,
 ):
     ctx, tp = lax.axis_index("ctx"), lax.axis_index("tp")
     n_ctx = lax.axis_size("ctx")
@@ -64,20 +64,21 @@
 
     greet(ctx, partner(1))
     greet(ctx, partner(2))
-    for d in range(1, NY):
-        greet(ctx - y + (y + NY - d) % NY, tp)
-
-    @pl.when(ctx > 0)
+
+    @pl.when(ctx < n_ctx - 1)
     def _():
         for s in range(4):
-            greet(ctx - 1, partner(s))
-
-    @pl.loop(0, g)
+            greet(ctx + 1, partner(s))
+
+    @pl.loop(y + 1, NY)
+    def _(k):
+        greet(g * NY + k, tp)
+
+    @pl.loop(g + 1, n_rows)
     def _(k):
         greet(k * NY + y, tp)
 
-    heard = 2 + (NY - 1) + 4 * jnp.where(ctx < n_ctx - 1, 1, 0) + (n_rows - 1 - g)
-    pl.semaphore_wait(barrier, heard)
+    pl.semaphore_wait(barrier, 2 + 4 * jnp.where(ctx > 0, 1, 0) + y + g)
 
     def sib_copy():
         return pltpu.make_async_remote_copy(
@@ -105,17 +106,28 @@
     for i in range(len(CHUNKS)):
         far_copy(i).start()
     sib_copy().start()
+
+    def answer(sem, c, t=tp):
+        pl.semaphore_signal(sem, inc=1, device_id={"ctx": c, "tp": t}, device_id_type=MESH)
+
+    @pl.when(ctx > 0)
+    def _():
+        for s in range(4):
+            answer(rim_ok, ctx - 1, partner(s))
+
+    @pl.loop(0, y)
+    def _(k):
+        answer(row_ok, g * NY + k)
+
+    @pl.loop(0, g)
+    def _(k):
+        answer(grid_ok, k * NY + y)
 
     tail_copy.wait()
     tail[...] = rim[...].astype(F32)
     for c in range(SUBL):
         pack[2 * c:2 * c + 2, :] = tail[14:16, c * LANE:(c + 1) * LANE]
     rim_out[...] = pack[...].astype(BF16)
-
-    @pl.when(ctx < n_ctx - 1)
-    def _():
-        for s in range(4):
-            rim_copy(s).start()
 
     for c in par_copies:
         c.wait()
@@ -143,60 +155,68 @@
     def _(b):
         power[b] = jnp.exp(-rate * (b + 1).astype(F32))
 
-    tail[...] = jnp.zeros_like(tail)
-    for s in range(4):
-        @pl.when(ctx > 0)
-        def _(s=s):
-            rim_copy(s).wait_recv()
-            pack[...] = rim_in[s].astype(F32)
-            for c in range(SUBL):
-                tail[14:16, c * LANE:(c + 1) * LANE] = pack[2 * c:2 * c + 2, :]
-
-        x[s, 0:HALO, :] = tail[...].astype(BF16)
-
     def tile_of(q):
-        return q // TILES, pl.ds(pl.multiple_of((q % TILES) * TILE, TILE), TILE)
+        return q // TILES, slice((q % TILES) * TILE, (q % TILES + 1) * TILE)
 
     own_copy.wait()
     for j in range(3):
         w_copy(0, j).wait()
 
-        @pl.loop(j * TILES, (j + 1) * TILES)
-        def _(q):
+        for q in range(j * TILES, (j + 1) * TILES):
             _, cols = tile_of(q)
-            acc[q] = jnp.dot(x[0], w[0, j, :, cols], preferred_element_type=F32)
+            acc[q, HALO:] = jnp.dot(x[0, HALO:], w[0, j, :, cols], preferred_element_type=F32)
+
+    @pl.when(ctx < n_ctx - 1)
+    def _():
+        pl.semaphore_wait(rim_ok, 4)
+        for s in range(4):
+            rim_copy(s).start()
 
     sib_copy().wait_recv()
     for j in range(3):
         w_copy(1, j).wait()
 
-        @pl.loop(j * TILES, (j + 1) * TILES)
-        def _(q):
+        for q in range(j * TILES, (j + 1) * TILES):
             _, cols = tile_of(q)
-            acc[q] += jnp.dot(x[1], w[1, j, :, cols], preferred_element_type=F32)
+            acc[q, HALO:] += jnp.dot(x[1, HALO:], w[1, j, :, cols], preferred_element_type=F32)
 
     def far_dots(i, q):
         j, cols = tile_of(q)
         first, size = CHUNKS[i]
         k = slice(first, first + size)
-        return (
-            jnp.dot(x[2, :, k], w[2, j, k, cols], preferred_element_type=F32)
-            + jnp.dot(x[3, :, k], w[3, j, k, cols], preferred_element_type=F32)
-        )
+        left = jnp.concatenate([x[2, :, k], x[3, :, k]], axis=1)
+        right = jnp.concatenate([w[2, j, k, cols], w[3, j, k, cols]], axis=0)
+        return jnp.dot(left, right, preferred_element_type=F32)
 
     last = len(CHUNKS) - 1
     for i in range(last + 1):
         far_copy(i).wait_recv()
         fwd_copy(i).start()
         if i == 0:
+            tail[...] = jnp.zeros_like(tail)
+            for s in range(4):
+                @pl.when(ctx > 0)
+                def _(s=s):
+                    rim_copy(s).wait_recv()
+                    pack[...] = rim_in[s].astype(F32)
+                    for c in range(SUBL):
+                        tail[14:16, c * LANE:(c + 1) * LANE] = pack[2 * c:2 * c + 2, :]
+
+                x[s, 0:HALO, :] = tail[...].astype(BF16)
+
+            for q in range(3 * TILES):
+                j, cols = tile_of(q)
+                acc[q, 0:HALO] = (
+                    jnp.dot(x[0, 0:HALO], w[0, j, :, cols], preferred_element_type=F32)
+                    + jnp.dot(x[1, 0:HALO], w[1, j, :, cols], preferred_element_type=F32)
+                )
             for s in (2, 3):
                 for j in range(3):
                     w_copy(s, j).wait()
         if i:
             fwd_copy(i - 1).wait_recv()
 
-            @pl.loop(0, 3 * TILES)
-            def _(q, i=i):
+            for q in range(3 * TILES):
                 acc[q] += far_dots(i - 1, q)
 
     def finish(q):
@@ -207,8 +227,7 @@
 
     fwd_copy(last).wait_recv()
 
-    @pl.loop(TILES, 3 * TILES)
-    def _(q):
+    for q in range(TILES, 3 * TILES):
         finish(q)
 
     def row(j, t):
@@ -250,11 +269,14 @@
             state, row_in.at[d - 1], row_s.at[d - 1], row_r.at[d - 1],
             device_id={"ctx": ctx - y + (y + d) % NY, "tp": tp}, device_id_type=MESH)
 
+    @pl.when(y < NY - 1)
+    def _():
+        pl.semaphore_wait(row_ok, NY - 1 - y)
+
     for d in range(1, NY):
         row_copy(d).start()
 
-    @pl.loop(0, TILES)
-    def _(q):
+    for q in range(TILES):
         finish(q)
 
     def local_step(i, carry):
@@ -269,8 +291,7 @@
             g1, g2 = g0, g1
         return s, g1, g2
 
-    half = ROWS // 16
-    carry = lax.fori_loop(0, half, local_step, (zero, row(0, -1), row(0, -2)))
+    lax.fori_loop(0, ROWS // 8, local_step, (zero, row(0, -1), row(0, -2)))
 
     prior, total = jnp.zeros((ORDER * SUBL, LANE), F32), row_tot[0]
     for d in range(1, NY):
@@ -279,20 +300,20 @@
         prior += wpre[d - 1] * got
         total += wtot[d] * got
     row_tot[0] = prior
-    for d in range(1, NY):
-        row_copy(d).wait_send()
-    state[...] = total.astype(BF16)
+    row_sum[...] = total.astype(BF16)
 
     def grid_copy(d):
         return pltpu.make_async_remote_copy(
-            state, grid_in.at[d - 1], grid_s.at[d - 1], grid_r.at[d - 1],
+            row_sum, grid_in.at[d - 1], grid_s.at[d - 1], grid_r.at[d - 1],
             device_id={"ctx": ctx + NY * d, "tp": tp}, device_id_type=MESH)
+
+    @pl.when(g < n_rows - 1)
+    def _():
+        pl.semaphore_wait(grid_ok, n_rows - 1 - g)
 
     @pl.loop(1, n_rows - g)
     def _(d):
         grid_copy(d).start()
-
-    lax.fori_loop(half, 2 * half, local_step, carry)
 
     def add_row(k, total):
         d = g - k
@@ -313,6 +334,8 @@
     for c in range(SUBL):
         out[:, c * LANE:(c + 1) * LANE] = base[pl.ds(c, ROWS, stride=SUBL), :].astype(BF16)
 
+    for d in range(1, NY):
+        row_copy(d).wait_send()
     sib_copy().wait_send()
     for i in range(last + 1):
         far_copy(i).wait_send()
@@ -336,7 +359,7 @@
     dma = pltpu.SemaphoreType.DMA
     return pl.pallas_call(
         kernel,
-        out_shape=jax.ShapeDtypeStruct((ROWS, WIDTH), BF16),
+        out_shape=pltpu.VMEM((ROWS, WIDTH), BF16),
         in_specs=[hbm] * 6,
         out_specs=pl.BlockSpec(memory_space=pltpu.VMEM),
         scratch_shapes=[
@@ -362,6 +385,7 @@
             pltpu.VMEM((ORDER, WIDTH), F32),
             pltpu.VMEM((SUBL, LANE), F32),
             pltpu.VMEM(flat, BF16),
+            pltpu.VMEM(flat, BF16),
             pltpu.VMEM((NY - 1, *flat), BF16),
             pltpu.VMEM((1, *flat), F32),
             pltpu.VMEM((n_rows - 1, *flat), BF16),
@@ -376,6 +400,7 @@
             dma((4,)), dma((4,)),
             dma((NY - 1,)), dma((NY - 1,)),
             dma((n_rows - 1,)), dma((n_rows - 1,)),
+            *[pltpu.SemaphoreType.REGULAR] * 3,
         ],
         compiler_params=pltpu.CompilerParams(
             collective_id=0, has_side_effects=True, vmem_limit_bytes=56 * 2**20),

time: 50.1 us -> 35.5 us (0.71)
  Pallas kernels: 47.4 us -> 34 us
  local copies, waits for them, and re-layouts: 1.87 us -> 0.8 us
    pallas_call x1, Pallas kernels: 47.4 us -> 34 us  [shards(): pl.pallas_call(kernel, out_shape=pltpu.VMEM((ROWS, WIDTH), BF16), in_spec...]
    unnamed x1, local copies, waits for them, and re-layouts: 1.87 us -> 0.8 us
where the time goes in v2:
time: 35.5 us; the launch traced here: 34.8 us
  Pallas kernels  34 us (96%)
  local copies, waits for them, and re-layouts  0.8 us (2%)
    pallas_call x1, Pallas kernels, shards(): pl.pallas_call(kernel, out_shape=pltpu.VMEM((ROWS, WIDTH), BF16), in_spec...  34 us
    unnamed x1, local copies, waits for them, and re-layouts  0.8 us

profile of v2, /device:TPU:96, one launch (start us, length us, event | category | flops | bytes accessed | tf_op | source)
XLA Modules:
  0.0 34.8 jit_solution(12781123630895113181)
XLA Ops:
  0.0 34.0 %hyena.1 = bf16[256,1024]{1,0:T(8,128)(2,1)S(1)} custom-call(bf16[256,1024]{1,0:T(8,128)(2,1)} %tokens.1, bf16[3,4096,1024]{2,1,0:T(8,128)(2,1)} %weight.1, f32[3,3,1024]{2,1,0:T(4,128)} %taps.1, f32[16,1024]{1,0:T(8,128)} %bitcast.3, f32[16,1024]{1,0:T(8,128)} %bitcast.4, f32[8,128]{1,0:T(8,128)} %bitcast.5), custom_call_target="tpu_custom_call" | custom-call | tf_op jit(solution)/shard_map/hyena/pallas_call | solution.py:360
  34.0 0.8 %copy.8 = bf16[256,1024]{1,0:T(8,128)(2,1)} copy(bf16[256,1024]{1,0:T(8,128)(2,1)S(1)} %hyena.1) | data formatting | bytes 1048576

commit v3 on v2

v3 whole, which is shorter than its diff:
```python
import jax
import jax.numpy as jnp
from jax import lax
from jax.experimental import pallas as pl
from jax.experimental.pallas import tpu as pltpu
from jax.sharding import PartitionSpec as P

MESH = pl.DeviceIdType.MESH
F32, BF16 = jnp.float32, jnp.bfloat16

ROWS = 256
HALF = 128
PAD = 8
M = PAD + ROWS + 2
WIDTH = 1024
ORDER = 16
LANE, SUBL = 128, 8
TILE = 256
TILES = WIDTH // TILE
NY = 4
STEP = 16
CHUNKS = (
    (0, 0, 512), (0, 512, 512),
    (HALF, 0, 512), (HALF, 512, 256), (HALF, 768, 128), (HALF, 896, 128),
)
EARLY = 2


def kernel(
    tokens, weight, taps, residues, rates, skip, out,
    w, x, acc, proj, src, base, gate, power, fac, fac_step, fac_inv, res, rim_out, rim_in, lead_out, lead_in,
    taps_v, taps_t, rates_v, res_v, skip_v, state, row_sum, row_in, row_tot, prior_own, grid_in, wpre, wtot,
    w_sem, tok_sem, par_sem, sib_s, sib_r, far_s, far_r, fwd_s, fwd_r,
    rim_s, rim_r, lead_s, lead_r, row_s, row_r, grid_s, grid_r, rim_ok, lead_ok, row_ok, grid_ok,
):
    ctx, tp = lax.axis_index("ctx"), lax.axis_index("tp")
    n_ctx = lax.axis_size("ctx")
    n_rows = n_ctx // NY
    y, g = ctx % NY, ctx // NY

    def partner(s):
        return (tp + 1 - 2 * (tp % 2), (tp + 2) % 4, 3 - tp)[s - 1] if s else tp

    def w_copy(s, j):
        rows = pl.ds(pl.multiple_of(partner(s) * WIDTH, WIDTH), WIDTH)
        return pltpu.make_async_copy(weight.at[j, rows, :], w.at[s, j], w_sem.at[s, j])

    own_copy = pltpu.make_async_copy(tokens, x.at[0], tok_sem)
    par_copies = [
        pltpu.make_async_copy(a, b, par_sem.at[i])
        for i, (a, b) in enumerate(
            ((taps, taps_v), (residues, res_v), (rates, rates_v), (skip, skip_v))
        )
    ]
    own_copy.start()
    for j in range(3):
        w_copy(0, j).start()
    for c in par_copies:
        c.start()
    for j in range(3):
        w_copy(1, j).start()

    barrier = pltpu.get_barrier_semaphore()

    def greet(c, t):
        pl.semaphore_signal(barrier, inc=1, device_id={"ctx": c, "tp": t}, device_id_type=MESH)

    greet(ctx, partner(1))
    greet(ctx, partner(2))

    @pl.when((y == 0) & (ctx > 0))
    def _():
        greet(ctx - 1, tp)

    @pl.loop(y + 1, NY)
    def _(k):
        greet(g * NY + k, tp)

    @pl.loop(g + 1, n_rows)
    def _(k):
        greet(k * NY + y, tp)

    pl.semaphore_wait(barrier, 2 + jnp.where((y == NY - 1) & (ctx < n_ctx - 1), 1, 0) + y + g)

    def sib_copy():
        return pltpu.make_async_remote_copy(
            tokens, x.at[1], sib_s, sib_r,
            device_id={"ctx": ctx, "tp": partner(1)}, device_id_type=MESH)

    def piece(i):
        first, column, columns = CHUNKS[i]
        return pl.ds(first, HALF), pl.ds(column, columns)

    def far_copy(i):
        return pltpu.make_async_remote_copy(
            tokens.at[piece(i)], x.at[2, *piece(i)], far_s.at[i], far_r.at[i],
            device_id={"ctx": ctx, "tp": partner(2)}, device_id_type=MESH)

    def fwd_copy(i):
        return pltpu.make_async_remote_copy(
            x.at[2, *piece(i)], x.at[3, *piece(i)], fwd_s.at[i], fwd_r.at[i],
            device_id={"ctx": ctx, "tp": partner(1)}, device_id_type=MESH)

    def rim_copy():
        return pltpu.make_async_remote_copy(
            rim_out, rim_in, rim_s, rim_r,
            device_id={"ctx": ctx + 1, "tp": tp}, device_id_type=MESH)

    def lead_copy():
        return pltpu.make_async_remote_copy(
            lead_out, lead_in, lead_s, lead_r,
            device_id={"ctx": ctx - 1, "tp": tp}, device_id_type=MESH)

    for i in range(len(CHUNKS)):
        far_copy(i).start()
    sib_copy().start()

    def answer(sem, c):
        pl.semaphore_signal(sem, inc=1, device_id={"ctx": c, "tp": tp}, device_id_type=MESH)

    @pl.when(y > 0)
    def _():
        answer(rim_ok, ctx - 1)

    @pl.when((y == NY - 1) & (ctx < n_ctx - 1))
    def _():
        answer(lead_ok, ctx + 1)

    @pl.loop(0, y)
    def _(k):
        answer(row_ok, g * NY + k)

    @pl.loop(0, g)
    def _(k):
        answer(grid_ok, k * NY + y)

    for c in par_copies:
        c.wait()

    def by_position(ref, first, value):
        count = value.shape[0]
        for c in range(SUBL):
            ref[pl.ds(first + c, count, stride=SUBL), :] = value[:, c * LANE:(c + 1) * LANE]

    for j in range(3):
        by_position(taps_t, j * 3 * SUBL, taps_v[j])
    by_position(res, 0, res_v[...])
    by_position(fac, 0, rates_v[...])
    rate = fac[...]
    for d in range(NY):
        below = (y + NY - d) % NY
        wtot[d] = jnp.exp(-rate * (ROWS * (NY - 1 - below)).astype(F32))
        if d:
            wpre[d - 1] = jnp.exp(-rate * float(ROWS * (d - 1))) * jnp.where(d <= y, 1.0, 0.0)
    fac_step[0] = jnp.exp(-rate * float(ROWS * NY))
    fac_step[1] = jnp.exp(-rate * (ROWS * y).astype(F32))
    fac_inv[...] = jnp.exp(rate)
    fac[...] = jnp.exp(-rate)

    @pl.loop(0, STEP)
    def _(b):
        power[b] = jnp.exp(-rate * (b + 1).astype(F32))

    for j in range(3):
        proj[j * M * SUBL:(j * M + PAD) * SUBL, :] = jnp.zeros((PAD * SUBL, LANE), F32)
        proj[((j + 1) * M - 2) * SUBL:(j + 1) * M * SUBL, :] = jnp.zeros((2 * SUBL, LANE), F32)

    def tile_of(q):
        return q // TILES, slice((q % TILES) * TILE, (q % TILES + 1) * TILE)

    own_copy.wait()
    for j in range(3):
        w_copy(0, j).wait()
        w_copy(2, j).start()
        for q in range(j * TILES, (j + 1) * TILES):
            _, cols = tile_of(q)
            acc[q] = jnp.dot(x[0], w[0, j, :, cols], preferred_element_type=F32)
    sib_copy().wait_recv()
    for j in range(3):
        w_copy(1, j).wait()
        w_copy(3, j).start()
        for q in range(j * TILES, (j + 1) * TILES):
            _, cols = tile_of(q)
            acc[q] += jnp.dot(x[1], w[1, j, :, cols], preferred_element_type=F32)

    def dots(i, q, slots):
        j, cols = tile_of(q)
        first, column, columns = CHUNKS[i]
        r, k = slice(first, first + HALF), slice(column, column + columns)
        left = jnp.concatenate([x[s, r, k] for s in slots], axis=1)
        right = jnp.concatenate([w[s, j, k, cols] for s in slots], axis=0)
        return jnp.dot(left, right, preferred_element_type=F32)

    def add(i, slots):
        r = slice(CHUNKS[i][0], CHUNKS[i][0] + HALF)
        for q in range(3 * TILES):
            acc[q, r] += dots(i, q, slots)

    def finish(i, q, slots):
        first = CHUNKS[i][0]
        value = acc[q, first:first + HALF] + dots(i, q, slots)
        value = value.astype(BF16).astype(F32)
        start = ((q // TILES) * M + PAD + first) * SUBL + (q % TILES) * (TILE // LANE)
        for c in range(TILE // LANE):
            proj[pl.ds(start + c, HALF, stride=SUBL), :] = value[:, c * LANE:(c + 1) * LANE]

    last = len(CHUNKS) - 1
    for i in range(EARLY):
        far_copy(i).wait_recv()
        fwd_copy(i).start()
        if i == 0:
            for j in range(3):
                w_copy(2, j).wait()
        add(i, (2,))
        if i == 0:
            for j in range(3):
                w_copy(3, j).wait()
        fwd_copy(i).wait_recv()
        if i < EARLY - 1:
            add(i, (3,))
    for q in range(3 * TILES):
        finish(EARLY - 1, q, (3,))

    def two_rows(j, t):
        first = (j * M + PAD + t) * SUBL
        return slice(first, first + 2 * SUBL)

    for j in (1, 2):
        lead_out[2 * SUBL * (j - 1):2 * SUBL * j, :] = proj[two_rows(j, 0), :].astype(BF16)

    @pl.when((y == 0) & (ctx > 0))
    def _():
        pl.semaphore_wait(lead_ok, 1)

    @pl.when(ctx > 0)
    def _():
        lead_copy().start()

    def row(j, t):
        first = (j * M + PAD + t) * SUBL
        return proj[pl.ds(pl.multiple_of(first, SUBL), SUBL), :]

    def at(t):
        return pl.ds(pl.multiple_of(t * SUBL, SUBL), SUBL)

    def tap(j, m):
        first = (j * 3 + m) * SUBL
        return taps_t[first:first + SUBL, :]

    shape, flat = (ORDER, SUBL, LANE), (ORDER * SUBL, LANE)

    def mix(j, p0, p1, p2):
        return tap(j, 0) * p0 + tap(j, 1) * p1 + tap(j, 2) * p2

    def source(keys, values):
        return (mix(1, *keys) * mix(2, *values)).astype(BF16).astype(F32)

    def source_at(t):
        return source([row(1, t - d) for d in range(3)], [row(2, t - d) for d in range(3)])

    def state_of(state, start, count, unroll):
        def state_step(i, carry):
            s, k1, k2, v1, v2 = carry
            f = fac[...].reshape(shape)
            for u in range(unroll):
                t = start + i * unroll + u
                k0, v0 = row(1, t), row(2, t)
                own = source((k0, k1, k2), (v0, v1, v2))
                src[at(t), :] = own
                s = f * s + own[None]
                k1, k2, v1, v2 = k0, k1, v0, v1
            return s, k1, k2, v1, v2

        before = [row(j, start - d) for j in (1, 2) for d in (1, 2)]
        return lax.fori_loop(0, count // unroll, state_step, (state, *before))[0]

    first_rows = fac[...].reshape(shape) * source_at(0)[None] + source_at(1)[None]
    first_rows = first_rows * jnp.where(ctx == 0, 1.0, 0.0)
    prior_own[...] = first_rows.reshape(flat)
    row_tot[0] = state_of(first_rows, 2, HALF - 2, 9).reshape(flat)

    for i in range(EARLY, last + 1):
        far_copy(i).wait_recv()
        fwd_copy(i).start()
        if i > EARLY:
            fwd_copy(i - 1).wait_recv()
            add(i - 1, (2, 3))
    fwd_copy(last).wait_recv()
    for q in range(TILES, 3 * TILES):
        finish(last, q, (2, 3))
    own_state = state_of(row_tot[0].reshape(shape), HALF, ROWS - HALF, 8)

    @pl.when(ctx < n_ctx - 1)
    def _():
        lead_copy().wait_recv()
        for j in (1, 2):
            proj[two_rows(j, ROWS), :] = lead_in[2 * SUBL * (j - 1):2 * SUBL * j, :].astype(F32)

    for t in (ROWS, ROWS + 1):
        own_state = fac[...].reshape(shape) * own_state + source_at(t)[None]
    own_state = own_state.reshape(flat)
    state[...] = own_state.astype(BF16)
    row_tot[0] = own_state * wtot[0]

    def row_copy(d):
        return pltpu.make_async_remote_copy(
            state, row_in.at[d - 1], row_s.at[d - 1], row_r.at[d - 1],
            device_id={"ctx": ctx - y + (y + d) % NY, "tp": tp}, device_id_type=MESH)

    @pl.when(y < NY - 1)
    def _():
        pl.semaphore_wait(row_ok, NY - 1 - y)

    for d in range(1, NY):
        row_copy(d).start()

    for q in range(TILES):
        finish(last, q, (2, 3))
    for j in range(3):
        rim_out[2 * SUBL * j:2 * SUBL * (j + 1), :] = proj[two_rows(j, ROWS - 2), :].astype(BF16)

    @pl.when(y < NY - 1)
    def _():
        pl.semaphore_wait(rim_ok, 1)

    @pl.when(ctx < n_ctx - 1)
    def _():
        rim_copy().start()

    def local_rows(first, count, carry):
        s, g1, g2 = carry
        f, r = fac[...].reshape(shape), res[...].reshape(shape)
        for u in range(count):
            t = first + u
            own, g0 = src[at(t), :], row(0, t)
            s = f * s + own[None]
            base[at(t), :] = jnp.sum(r * s, axis=0) + skip_v[...] * own
            gate[at(t), :] = mix(0, g0, g1, g2)
            g1, g2 = g0, g1
        return s, g1, g2

    carry = lax.fori_loop(
        0, (ROWS - 2) // 8, lambda i, carry: local_rows(2 + i * 8, 8, carry),
        (jnp.zeros(shape, F32), row(0, 1), row(0, 0)))
    local_rows(2 + (ROWS - 2) // 8 * 8, (ROWS - 2) % 8, carry)

    prior, total = jnp.zeros(flat, F32), row_tot[0]
    for d in range(1, NY):
        row_copy(d).wait_recv()
        got = row_in[d - 1].astype(F32)
        prior += wpre[d - 1] * got
        total += wtot[d] * got
    row_tot[0] = prior
    row_sum[...] = total.astype(BF16)

    def grid_copy(d):
        return pltpu.make_async_remote_copy(
            row_sum, grid_in.at[d - 1], grid_s.at[d - 1], grid_r.at[d - 1],
            device_id={"ctx": ctx + NY * d, "tp": tp}, device_id_type=MESH)

    @pl.when(g < n_rows - 1)
    def _():
        pl.semaphore_wait(grid_ok, n_rows - 1 - g)

    @pl.loop(1, n_rows - g)
    def _(d):
        grid_copy(d).start()

    @pl.when(ctx > 0)
    def _():
        rim_copy().wait_recv()
        for j in range(3):
            proj[two_rows(j, -2), :] = rim_in[2 * SUBL * j:2 * SUBL * (j + 1), :].astype(F32)

    for t in (0, 1):
        src[at(t), :] = source_at(t)
        base[at(t), :] = skip_v[...] * src[at(t), :]
        gate[at(t), :] = mix(0, *[row(0, t - d) for d in range(3)])

    def add_row(k, total):
        d = g - k
        grid_copy(d).wait_recv()
        return fac_step[0] * total + grid_in[d - 1].astype(F32)

    ahead = lax.fori_loop(0, g, add_row, jnp.zeros(flat, F32))
    ahead = row_tot[0] + fac_step[1] * ahead + prior_own[...]

    def close(t, conv):
        base[at(t), :] = gate[at(t), :] * (conv + base[at(t), :])

    weighted = (res[...] * ahead).reshape(shape)
    close(1, jnp.sum(weighted, axis=0))
    before = (ahead.reshape(shape) - src[at(1), :][None]) * fac_inv[...].reshape(shape)
    close(0, jnp.sum(res[...].reshape(shape) * before, axis=0))

    def last_rows(first, count, u):
        for b in range(count):
            close(first + b, jnp.sum(u * power[b].reshape(shape), axis=0))

    def last_step(a, u):
        last_rows(2 + a * STEP, STEP, u)
        return u * power[STEP - 1].reshape(shape)

    whole = (ROWS - 2) // STEP
    weighted = lax.fori_loop(0, whole, last_step, weighted)
    last_rows(2 + whole * STEP, ROWS - 2 - whole * STEP, weighted)
    for c in range(SUBL):
        out[:, c * LANE:(c + 1) * LANE] = base[pl.ds(c, ROWS, stride=SUBL), :].astype(BF16)

    for d in range(1, NY):
        row_copy(d).wait_send()
    sib_copy().wait_send()
    for i in range(last + 1):
        far_copy(i).wait_send()
        fwd_copy(i).wait_send()

    @pl.when(ctx < n_ctx - 1)
    def _():
        rim_copy().wait_send()

    @pl.when(ctx > 0)
    def _():
        lead_copy().wait_send()

    @pl.loop(1, n_rows - g)
    def _(d):
        grid_copy(d).wait_send()


def shards(tokens, proj_weight, short_taps, residues, rates, skip):
    hbm = pl.BlockSpec(memory_space=pltpu.HBM)
    n_rows = lax.axis_size("ctx") // NY
    chunks = len(CHUNKS)
    flat = (ORDER * SUBL, LANE)
    dma = pltpu.SemaphoreType.DMA
    return pl.pallas_call(
        kernel,
        out_shape=pltpu.VMEM((ROWS, WIDTH), BF16),
        in_specs=[hbm] * 6,
        out_specs=pl.BlockSpec(memory_space=pltpu.VMEM),
        scratch_shapes=[
            pltpu.VMEM((4, 3, WIDTH, WIDTH), BF16),
            pltpu.VMEM((4, ROWS, WIDTH), BF16),
            pltpu.VMEM((3 * TILES, ROWS, TILE), F32),
            pltpu.VMEM((3 * M * SUBL, LANE), F32),
            pltpu.VMEM((ROWS * SUBL, LANE), F32),
            pltpu.VMEM((ROWS * SUBL, LANE), F32),
            pltpu.VMEM((ROWS * SUBL, LANE), F32),
            pltpu.VMEM((STEP, *flat), F32),
            pltpu.VMEM(flat, F32),
            pltpu.VMEM((2, *flat), F32),
            pltpu.VMEM(flat, F32),
            pltpu.VMEM(flat, F32),
            pltpu.VMEM((3 * 2 * SUBL, LANE), BF16),
            pltpu.VMEM((3 * 2 * SUBL, LANE), BF16),
            pltpu.VMEM((2 * 2 * SUBL, LANE), BF16),
            pltpu.VMEM((2 * 2 * SUBL, LANE), BF16),
            pltpu.VMEM((3, 3, WIDTH), F32),
            pltpu.VMEM((9 * SUBL, LANE), F32),
            pltpu.VMEM((ORDER, WIDTH), F32),
            pltpu.VMEM((ORDER, WIDTH), F32),
            pltpu.VMEM((SUBL, LANE), F32),
            pltpu.VMEM(flat, BF16),
            pltpu.VMEM(flat, BF16),
            pltpu.VMEM((NY - 1, *flat), BF16),
            pltpu.VMEM((1, *flat), F32),
            pltpu.VMEM(flat, F32),
            pltpu.VMEM((n_rows - 1, *flat), BF16),
            pltpu.VMEM((NY - 1, *flat), F32),
            pltpu.VMEM((NY, *flat), F32),
            dma((4, 3)),
            dma,
            dma((4,)),
            dma, dma,
            dma((chunks,)), dma((chunks,)),
            dma((chunks,)), dma((chunks,)),
            dma, dma,
            dma, dma,
            dma((NY - 1,)), dma((NY - 1,)),
            dma((n_rows - 1,)), dma((n_rows - 1,)),
            *[pltpu.SemaphoreType.REGULAR] * 4,
        ],
        compiler_params=pltpu.CompilerParams(
            collective_id=0, has_side_effects=True, vmem_limit_bytes=56 * 2**20),
        name="hyena",
    )(tokens, proj_weight, short_taps, residues.T, rates.T, skip.reshape(SUBL, LANE))


def solution(mesh):
    return jax.shard_map(
        shards,
        mesh=mesh,
        in_specs=(
            P("ctx", "tp"),
            P(None, None, "tp"),
            P(None, None, "tp"),
            P("tp", None),
            P("tp", None),
            P("tp"),
        ),
        out_specs=P("ctx", "tp"),
        check_vma=False,
    )
```

time: 35.5 us -> 32 us (0.901); the launches traced: 34.8 us -> 31.9 us
  Pallas kernels: 34 us -> 31.1 us
    pallas_call x1, Pallas kernels: 34 us -> 31.1 us  [shards(): pl.pallas_call(kernel, out_shape=pltpu.VMEM((ROWS, WIDTH), BF16), in_spec...]
where the time goes in v3:
time: 32 us; the launch traced here: 31.9 us
  Pallas kernels  31.1 us (97%)
  local copies, waits for them, and re-layouts  0.8 us (2%)
    pallas_call x1, Pallas kernels, shards(): pl.pallas_call(kernel, out_shape=pltpu.VMEM((ROWS, WIDTH), BF16), in_spec...  31.1 us
    unnamed x1, local copies, waits for them, and re-layouts  0.8 us

profile of v3, /device:TPU:96, one launch (start us, length us, event | category | flops | bytes accessed | tf_op | source)
XLA Modules:
  0.0 31.9 jit_solution(6768925107755859029)
XLA Ops:
  0.0 31.1 %hyena.1 = bf16[256,1024]{1,0:T(8,128)(2,1)S(1)} custom-call(bf16[256,1024]{1,0:T(8,128)(2,1)} %tokens.1, bf16[3,4096,1024]{2,1,0:T(8,128)(2,1)} %weight.1, f32[3,3,1024]{2,1,0:T(4,128)} %taps.1, f32[16,1024]{1,0:T(8,128)} %bitcast.3, f32[16,1024]{1,0:T(8,128)} %bitcast.4, f32[8,128]{1,0:T(8,128)} %bitcast.5), custom_call_target="tpu_custom_call" | custom-call | tf_op jit(solution)/shard_map/hyena/pallas_call | solution.py:436
  31.1 0.8 %copy.8 = bf16[256,1024]{1,0:T(8,128)(2,1)} copy(bf16[256,1024]{1,0:T(8,128)(2,1)S(1)} %hyena.1) | data formatting | bytes 1048576

commit v4 on v3

v4 whole, which is shorter than its diff:
```python
import jax
import jax.numpy as jnp
from jax import lax
from jax.experimental import pallas as pl
from jax.experimental.pallas import tpu as pltpu
from jax.sharding import PartitionSpec as P

MESH = pl.DeviceIdType.MESH
F32, BF16 = jnp.float32, jnp.bfloat16

ROWS = 256
HALF = 128
PAD = 8
M = PAD + ROWS
WIDTH = 1024
ORDER = 16
LANE, SUBL = 128, 8
TILE = 256
TILES = WIDTH // TILE
NY = 4
STEP = 16
CHUNKS = (
    (HALF, 0, 512), (HALF, 512, 512),
    (0, 0, 512), (0, 512, 256), (0, 768, 128), (0, 896, 128),
)
LATER = 2


def kernel(
    tokens, weight, taps, residues, rates, skip, out,
    w, x, acc, proj, src, base, gate, done, power, fac, fac_step, fac_part, res, rim_out, rim_in,
    taps_v, taps_t, rates_v, res_v, skip_v, state, row_sum, row_in, row_tot, grid_in, wpre, wtot,
    w_sem, tok_sem, par_sem, sib_s, sib_r, far_s, far_r, fwd_s, fwd_r, cross_s, cross_r,
    rim_s, rim_r, row_s, row_r, grid_s, grid_r, rim_ok, row_ok, grid_ok, seam_ok,
):
    ctx, tp = lax.axis_index("ctx"), lax.axis_index("tp")
    n_ctx = lax.axis_size("ctx")
    n_rows = n_ctx // NY
    y, g = ctx % NY, ctx // NY
    nx = n_rows // 2
    half, xx = g // nx, g % nx
    seam = nx * NY

    def partner(s):
        return (tp + 1 - 2 * (tp % 2), (tp + 2) % 4, 3 - tp)[s - 1] if s else tp

    def w_copy(s, j):
        rows = pl.ds(pl.multiple_of(partner(s) * WIDTH, WIDTH), WIDTH)
        return pltpu.make_async_copy(weight.at[j, rows, :], w.at[s, j], w_sem.at[s, j])

    own_copy = pltpu.make_async_copy(tokens, x.at[0], tok_sem)
    par_copies = [
        pltpu.make_async_copy(a, b, par_sem.at[i])
        for i, (a, b) in enumerate(
            ((taps, taps_v), (residues, res_v), (rates, rates_v), (skip, skip_v))
        )
    ]
    barrier = pltpu.get_barrier_semaphore()

    def greet(c, t):
        pl.semaphore_signal(barrier, inc=1, device_id={"ctx": c, "tp": t}, device_id_type=MESH)

    greet(ctx, partner(1))
    greet(ctx, partner(2))
    greet(ctx, partner(3))

    @pl.when((y == 0) & (xx > 0))
    def _():
        greet(ctx - 1, tp)

    @pl.loop(y + 1, NY)
    def _(k):
        greet(g * NY + k, tp)

    @pl.loop(xx + 1, nx)
    def _(k):
        greet((half * nx + k) * NY + y, tp)

    @pl.when(half == 0)
    def _():
        @pl.loop(xx, nx)
        def _(k):
            greet((nx + k) * NY + y, tp)

    own_copy.start()
    for j in range(3):
        w_copy(0, j).start()
    for c in par_copies:
        c.start()
    for j in range(3):
        w_copy(1, j).start()

    heard = 3 + jnp.where((y == NY - 1) & (xx < nx - 1), 1, 0) + y + xx + half * (xx + 1)
    pl.semaphore_wait(barrier, heard)

    def sib_copy():
        return pltpu.make_async_remote_copy(
            tokens, x.at[1], sib_s, sib_r,
            device_id={"ctx": ctx, "tp": partner(1)}, device_id_type=MESH)

    def piece(i):
        first, column, columns = CHUNKS[i]
        return pl.ds(first, HALF), pl.ds(column, columns)

    def far_copy(i):
        return pltpu.make_async_remote_copy(
            tokens.at[piece(i)], x.at[2, *piece(i)], far_s.at[i], far_r.at[i],
            device_id={"ctx": ctx, "tp": partner(2)}, device_id_type=MESH)

    def fwd_copy(i):
        return pltpu.make_async_remote_copy(
            x.at[2, *piece(i)], x.at[3, *piece(i)], fwd_s.at[i], fwd_r.at[i],
            device_id={"ctx": ctx, "tp": partner(1)}, device_id_type=MESH)

    def cross_copy():
        return pltpu.make_async_remote_copy(
            tokens.at[piece(len(CHUNKS) - 1)], x.at[3, *piece(len(CHUNKS) - 1)], cross_s, cross_r,
            device_id={"ctx": ctx, "tp": partner(3)}, device_id_type=MESH)

    def rim_copy():
        return pltpu.make_async_remote_copy(
            rim_out, rim_in, rim_s, rim_r,
            device_id={"ctx": ctx + 1, "tp": tp}, device_id_type=MESH)

    for i in range(len(CHUNKS)):
        far_copy(i).start()
    cross_copy().start()
    sib_copy().start()

    def answer(sem, c):
        pl.semaphore_signal(sem, inc=1, device_id={"ctx": c, "tp": tp}, device_id_type=MESH)

    @pl.when(y > 0)
    def _():
        answer(rim_ok, ctx - 1)

    @pl.loop(0, y)
    def _(k):
        answer(row_ok, g * NY + k)

    @pl.loop(0, xx)
    def _(k):
        answer(grid_ok, (half * nx + k) * NY + y)

    @pl.when(half == 1)
    def _():
        @pl.loop(0, xx + 1)
        def _(k):
            answer(grid_ok, k * NY + y)

    for c in par_copies:
        c.wait()

    def by_position(ref, first, value):
        count = value.shape[0]
        for c in range(SUBL):
            ref[pl.ds(first + c, count, stride=SUBL), :] = value[:, c * LANE:(c + 1) * LANE]

    for j in range(3):
        by_position(taps_t, j * 3 * SUBL, taps_v[j])
    by_position(res, 0, res_v[...])
    by_position(fac, 0, rates_v[...])
    rate = fac[...]
    for d in range(NY):
        below = (y + NY - d) % NY
        wtot[d] = jnp.exp(-rate * (ROWS * (NY - 1 - below)).astype(F32))
        if d:
            wpre[d - 1] = jnp.exp(-rate * float(ROWS * (d - 1))) * jnp.where(d <= y, 1.0, 0.0)
    fac_step[0] = jnp.exp(-rate * float(ROWS * NY))
    fac_step[1] = jnp.exp(-rate * (ROWS * y).astype(F32))
    fac_part[0] = jnp.exp(-rate * float(ROWS - 2))
    fac_part[1] = jnp.exp(-rate * float(ROWS - HALF - 2))
    fac[...] = jnp.exp(-rate)

    @pl.loop(0, STEP)
    def _(b):
        power[b] = jnp.exp(-rate * (b + 1).astype(F32))

    for j in range(3):
        proj[j * M * SUBL:(j * M + PAD) * SUBL, :] = jnp.zeros((PAD * SUBL, LANE), F32)

    def tile_of(q):
        return q // TILES, slice((q % TILES) * TILE, (q % TILES + 1) * TILE)

    own_copy.wait()
    for j in range(3):
        w_copy(0, j).wait()
        w_copy(2, j).start()
        for q in range(j * TILES, (j + 1) * TILES):
            _, cols = tile_of(q)
            acc[q] = jnp.dot(x[0], w[0, j, :, cols], preferred_element_type=F32)
    @pl.when((half == 1) & (xx < nx - 1))
    def _():
        pl.semaphore_wait(grid_ok, nx - 1 - xx)

        @pl.loop(xx + 1, nx)
        def _(k):
            answer(grid_ok, k * NY + y)

    @pl.when(ctx == seam)
    def _():
        answer(seam_ok, seam - NY)

    sib_copy().wait_recv()
    for j in range(3):
        w_copy(1, j).wait()
        w_copy(3, j).start()
        for q in range(j * TILES, (j + 1) * TILES):
            _, cols = tile_of(q)
            acc[q] += jnp.dot(x[1], w[1, j, :, cols], preferred_element_type=F32)

    @pl.when(y < NY - 1)
    def _():
        pl.semaphore_wait(row_ok, NY - 1 - y)

    @pl.when(ctx == seam - NY)
    def _():
        pl.semaphore_wait(seam_ok, 1)
        answer(rim_ok, seam - 1)

    def dots(i, q, slots):
        j, cols = tile_of(q)
        first, column, columns = CHUNKS[i]
        r, k = slice(first, first + HALF), slice(column, column + columns)
        left = jnp.concatenate([x[s, r, k] for s in slots], axis=1)
        right = jnp.concatenate([w[s, j, k, cols] for s in slots], axis=0)
        return jnp.dot(left, right, preferred_element_type=F32)

    def add(i, slots):
        r = slice(CHUNKS[i][0], CHUNKS[i][0] + HALF)
        for q in range(3 * TILES):
            acc[q, r] += dots(i, q, slots)

    def finish(i, q, slots):
        first = CHUNKS[i][0]
        value = acc[q, first:first + HALF] + dots(i, q, slots)
        value = value.astype(BF16).astype(F32)
        start = ((q // TILES) * M + PAD + first) * SUBL + (q % TILES) * (TILE // LANE)
        for c in range(TILE // LANE):
            proj[pl.ds(start + c, HALF, stride=SUBL), :] = value[:, c * LANE:(c + 1) * LANE]

    last = len(CHUNKS) - 1
    for i in range(LATER):
        far_copy(i).wait_recv()
        fwd_copy(i).start()
        if i == 0:
            for j in range(3):
                w_copy(2, j).wait()
        add(i, (2,))
        if i == 0:
            for j in range(3):
                w_copy(3, j).wait()
        fwd_copy(i).wait_recv()
        if i < LATER - 1:
            add(i, (3,))
    for q in range(3 * TILES):
        finish(LATER - 1, q, (3,))

    for j in range(3):
        first = ((j + 1) * M - 2) * SUBL
        rim_out[2 * SUBL * j:2 * SUBL * (j + 1), :] = proj[first:first + 2 * SUBL, :].astype(BF16)

    @pl.when((y < NY - 1) | (ctx == seam - 1))
    def _():
        pl.semaphore_wait(rim_ok, 1)

    @pl.when(ctx < n_ctx - 1)
    def _():
        rim_copy().start()

    def row(j, t):
        first = (j * M + PAD + t) * SUBL
        return proj[pl.ds(pl.multiple_of(first, SUBL), SUBL), :]

    def at(t):
        return pl.ds(pl.multiple_of(t * SUBL, SUBL), SUBL)

    def tap(j, m):
        first = (j * 3 + m) * SUBL
        return taps_t[first:first + SUBL, :]

    shape, flat = (ORDER, SUBL, LANE), (ORDER * SUBL, LANE)

    def mix(j, p0, p1, p2):
        return tap(j, 0) * p0 + tap(j, 1) * p1 + tap(j, 2) * p2

    def own_source(t, keys, values):
        own = (mix(1, *keys) * mix(2, *values)).astype(BF16).astype(F32)
        src[at(t), :] = own
        return own

    zero = jnp.zeros(shape, F32)

    def state_of(start, count, unroll):
        def state_step(i, carry):
            s, k1, k2, v1, v2 = carry
            f = fac[...].reshape(shape)
            for u in range(unroll):
                t = start + i * unroll + u
                k0, v0 = row(1, t), row(2, t)
                s = f * s + own_source(t, (k0, k1, k2), (v0, v1, v2))[None]
                k1, k2, v1, v2 = k0, k1, v0, v1
            return s, k1, k2, v1, v2

        before = [row(j, start - d) for j in (1, 2) for d in (1, 2)]
        return lax.fori_loop(0, count // unroll, state_step, (zero, *before))[0]

    later_state = state_of(HALF + 2, HALF - 2, 9)
    row_tot[0] = later_state.reshape(flat)

    for i in range(LATER, last + 1):
        far_copy(i).wait_recv()
        if i < last:
            fwd_copy(i).start()
        if i > LATER:
            fwd_copy(i - 1).wait_recv()
            add(i - 1, (2, 3))
    cross_copy().wait_recv()
    for q in range(TILES, 3 * TILES):
        finish(last, q, (2, 3))
    early_state = state_of(2, HALF, 8)

    @pl.when(ctx > 0)
    def _():
        rim_copy().wait_recv()
        for j in range(3):
            first = (j * M + PAD - 2) * SUBL
            proj[first:first + 2 * SUBL, :] = rim_in[2 * SUBL * j:2 * SUBL * (j + 1), :].astype(F32)

    rim_state = fac[...].reshape(shape) * own_source(
        0, [row(1, -d) for d in range(3)], [row(2, -d) for d in range(3)])[None]
    rim_state += own_source(
        1, [row(1, 1 - d) for d in range(3)], [row(2, 1 - d) for d in range(3)])[None]
    own_state = row_tot[0] + fac_part[1] * early_state.reshape(flat)
    own_state += fac_part[0] * rim_state.reshape(flat)
    state[...] = own_state.astype(BF16)

    def row_copy(d):
        return pltpu.make_async_remote_copy(
            state, row_in.at[d - 1], row_s.at[d - 1], row_r.at[d - 1],
            device_id={"ctx": ctx - y + (y + d) % NY, "tp": tp}, device_id_type=MESH)

    for d in (2, 1, 3):
        row_copy(d).start()
    row_tot[0] = own_state * wtot[0]

    for q in range(TILES):
        finish(last, q, (2, 3))

    def local_step(i, carry):
        s, g1, g2 = carry
        f, r = fac[...].reshape(shape), res[...].reshape(shape)
        for u in range(8):
            t = i * 8 + u
            own, g0 = src[at(t), :], row(0, t)
            s = f * s + own[None]
            base[at(t), :] = jnp.sum(r * s, axis=0) + skip_v[...] * own
            gate[at(t), :] = tap(0, 0) * g0 + tap(0, 1) * g1 + tap(0, 2) * g2
            g1, g2 = g0, g1
        return s, g1, g2

    lax.fori_loop(0, ROWS // 8, local_step, (zero, row(0, -1), row(0, -2)))

    total = row_tot[0]
    for d in range(1, NY):
        row_copy(d).wait_recv()
        total += wtot[d] * row_in[d - 1].astype(F32)
    row_sum[...] = total.astype(BF16)

    def grid_copy(d):
        return pltpu.make_async_remote_copy(
            row_sum, grid_in.at[d - 1], grid_s.at[d - 1], grid_r.at[d - 1],
            device_id={"ctx": ctx + NY * d, "tp": tp}, device_id_type=MESH)

    @pl.when(half == 0)
    def _():
        pl.semaphore_wait(grid_ok, n_rows - 1 - g)

    for d in range(1, n_rows):
        @pl.when(d < n_rows - g)
        def _(d=d):
            grid_copy(d).start()

    prior = jnp.zeros(flat, F32)
    for d in range(1, NY):
        prior += wpre[d - 1] * row_in[d - 1].astype(F32)
    row_tot[0] = prior

    for d in range(1, NY):
        row_copy(d).wait_send()
    sib_copy().wait_send()
    for i in range(last + 1):
        far_copy(i).wait_send()
        if i < last:
            fwd_copy(i).wait_send()
    cross_copy().wait_send()

    @pl.when(ctx < n_ctx - 1)
    def _():
        rim_copy().wait_send()

    def add_row(k, total):
        d = g - k
        grid_copy(d).wait_recv()
        return fac_step[0] * total + grid_in[d - 1].astype(F32)

    ahead = lax.fori_loop(0, g, add_row, jnp.zeros(flat, F32))
    ahead = row_tot[0] + fac_step[1] * ahead

    def last_rows(first, u):
        for b in range(STEP):
            t = first + b
            conv = jnp.sum(u * power[b].reshape(shape), axis=0)
            done[at(t), :] = gate[at(t), :] * (conv + base[at(t), :])
        return u * power[STEP - 1].reshape(shape)

    def emit(a):
        rows = pl.ds(pl.multiple_of(a * STEP, STEP), STEP)
        for c in range(SUBL):
            value = done[pl.ds(a * STEP * SUBL + c, STEP, stride=SUBL), :]
            out[rows, c * LANE:(c + 1) * LANE] = value.astype(BF16)

    def last_step(a, u):
        emit(a - 1)
        return last_rows(a * STEP, u)

    weighted = last_rows(0, (res[...] * ahead).reshape(shape))
    lax.fori_loop(1, ROWS // STEP, last_step, weighted)
    emit(ROWS // STEP - 1)

    @pl.loop(1, n_rows - g)
    def _(d):
        grid_copy(d).wait_send()


def shards(tokens, proj_weight, short_taps, residues, rates, skip):
    hbm = pl.BlockSpec(memory_space=pltpu.HBM)
    n_rows = lax.axis_size("ctx") // NY
    chunks = len(CHUNKS)
    flat = (ORDER * SUBL, LANE)
    dma = pltpu.SemaphoreType.DMA
    return pl.pallas_call(
        kernel,
        out_shape=pltpu.VMEM((ROWS, WIDTH), BF16),
        in_specs=[hbm] * 6,
        out_specs=pl.BlockSpec(memory_space=pltpu.VMEM),
        scratch_shapes=[
            pltpu.VMEM((4, 3, WIDTH, WIDTH), BF16),
            pltpu.VMEM((4, ROWS, WIDTH), BF16),
            pltpu.VMEM((3 * TILES, ROWS, TILE), F32),
            pltpu.VMEM((3 * M * SUBL, LANE), F32),
            pltpu.VMEM((ROWS * SUBL, LANE), F32),
            pltpu.VMEM((ROWS * SUBL, LANE), F32),
            pltpu.VMEM((ROWS * SUBL, LANE), F32),
            pltpu.VMEM((ROWS * SUBL, LANE), F32),
            pltpu.VMEM((STEP, *flat), F32),
            pltpu.VMEM(flat, F32),
            pltpu.VMEM((2, *flat), F32),
            pltpu.VMEM((2, *flat), F32),
            pltpu.VMEM(flat, F32),
            pltpu.VMEM((3 * 2 * SUBL, LANE), BF16),
            pltpu.VMEM((3 * 2 * SUBL, LANE), BF16),
            pltpu.VMEM((3, 3, WIDTH), F32),
            pltpu.VMEM((9 * SUBL, LANE), F32),
            pltpu.VMEM((ORDER, WIDTH), F32),
            pltpu.VMEM((ORDER, WIDTH), F32),
            pltpu.VMEM((SUBL, LANE), F32),
            pltpu.VMEM(flat, BF16),
            pltpu.VMEM(flat, BF16),
            pltpu.VMEM((NY - 1, *flat), BF16),
            pltpu.VMEM((1, *flat), F32),
            pltpu.VMEM((n_rows - 1, *flat), BF16),
            pltpu.VMEM((NY - 1, *flat), F32),
            pltpu.VMEM((NY, *flat), F32),
            dma((4, 3)),
            dma,
            dma((4,)),
            dma, dma,
            dma((chunks,)), dma((chunks,)),
            dma((chunks - 1,)), dma((chunks - 1,)),
            dma, dma,
            dma, dma,
            dma((NY - 1,)), dma((NY - 1,)),
            dma((n_rows - 1,)), dma((n_rows - 1,)),
            *[pltpu.SemaphoreType.REGULAR] * 4,
        ],
        compiler_params=pltpu.CompilerParams(
            collective_id=0, has_side_effects=True, vmem_limit_bytes=56 * 2**20),
        name="hyena",
    )(tokens, proj_weight, short_taps, residues.T, rates.T, skip.reshape(SUBL, LANE))


def solution(mesh):
    return jax.shard_map(
        shards,
        mesh=mesh,
        in_specs=(
            P("ctx", "tp"),
            P(None, None, "tp"),
            P(None, None, "tp"),
            P("tp", None),
            P("tp", None),
            P("tp"),
        ),
        out_specs=P("ctx", "tp"),
        check_vma=False,
    )
```

time: 32 us -> 31.6 us (0.988)
  Pallas kernels: 31.1 us -> 30.6 us
    pallas_call x1, Pallas kernels: 31.1 us -> 30.6 us  [shards(): pl.pallas_call(kernel, out_shape=pltpu.VMEM((ROWS, WIDTH), BF16), in_spec...]
where the time goes in v4:
time: 31.6 us; the launch traced here: 31.4 us
  Pallas kernels  30.6 us (97%)
  local copies, waits for them, and re-layouts  0.8 us (3%)
    pallas_call x1, Pallas kernels, shards(): pl.pallas_call(kernel, out_shape=pltpu.VMEM((ROWS, WIDTH), BF16), in_spec...  30.6 us
    unnamed x1, local copies, waits for them, and re-layouts  0.8 us

profile of v4, /device:TPU:96, one launch (start us, length us, event | category | flops | bytes accessed | tf_op | source)
XLA Modules:
  0.0 31.4 jit_solution(4297757778686550729)
XLA Ops:
  0.0 30.6 %hyena.1 = bf16[256,1024]{1,0:T(8,128)(2,1)S(1)} custom-call(bf16[256,1024]{1,0:T(8,128)(2,1)} %tokens.1, bf16[3,4096,1024]{2,1,0:T(8,128)(2,1)} %weight.1, f32[3,3,1024]{2,1,0:T(4,128)} %taps.1, f32[16,1024]{1,0:T(8,128)} %bitcast.3, f32[16,1024]{1,0:T(8,128)} %bitcast.4, f32[8,128]{1,0:T(8,128)} %bitcast.5), custom_call_target="tpu_custom_call" | custom-call | tf_op jit(solution)/shard_map/hyena/pallas_call | solution.py:442
  30.6 0.8 %copy.8 = bf16[256,1024]{1,0:T(8,128)(2,1)} copy(bf16[256,1024]{1,0:T(8,128)(2,1)S(1)} %hyena.1) | data formatting | bytes 1048576

commit v5 on v4

--- a/solution.py
+++ b/solution.py
@@ -28,7 +28,7 @@
 
 def kernel(
     tokens, weight, taps, residues, rates, skip, out,
-    w, x, acc, proj, src, base, gate, done, power, fac, fac_step, fac_part, res, rim_out, rim_in,
+    w, x, acc, proj, src, base, gate, done, fac, fac_step, fac_part, res, rim_out, rim_in,
     taps_v, taps_t, rates_v, res_v, skip_v, state, row_sum, row_in, row_tot, grid_in, wpre, wtot,
     w_sem, tok_sem, par_sem, sib_s, sib_r, far_s, far_r, fwd_s, fwd_r, cross_s, cross_r,
     rim_s, rim_r, row_s, row_r, grid_s, grid_r, rim_ok, row_ok, grid_ok, seam_ok,
@@ -172,10 +172,6 @@
     fac_part[1] = jnp.exp(-rate * float(ROWS - HALF - 2))
     fac[...] = jnp.exp(-rate)
 
-    @pl.loop(0, STEP)
-    def _(b):
-        power[b] = jnp.exp(-rate * (b + 1).astype(F32))
-
     for j in range(3):
         proj[j * M * SUBL:(j * M + PAD) * SUBL, :] = jnp.zeros((PAD * SUBL, LANE), F32)
 
@@ -226,9 +222,9 @@
         right = jnp.concatenate([w[s, j, k, cols] for s in slots], axis=0)
         return jnp.dot(left, right, preferred_element_type=F32)
 
-    def add(i, slots):
+    def add(i, slots, tiles=range(3 * TILES)):
         r = slice(CHUNKS[i][0], CHUNKS[i][0] + HALF)
-        for q in range(3 * TILES):
+        for q in tiles:
             acc[q, r] += dots(i, q, slots)
 
     def finish(i, q, slots):
@@ -314,7 +310,7 @@
             fwd_copy(i).start()
         if i > LATER:
             fwd_copy(i - 1).wait_recv()
-            add(i - 1, (2, 3))
+            add(i - 1, (2, 3), range(0 if i < last else TILES, 3 * TILES))
     cross_copy().wait_recv()
     for q in range(TILES, 3 * TILES):
         finish(last, q, (2, 3))
@@ -344,6 +340,7 @@
         row_copy(d).start()
     row_tot[0] = own_state * wtot[0]
 
+    add(last - 1, (2, 3), range(TILES))
     for q in range(TILES):
         finish(last, q, (2, 3))
 
@@ -408,11 +405,12 @@
     ahead = row_tot[0] + fac_step[1] * ahead
 
     def last_rows(first, u):
+        f = fac[...].reshape(shape)
         for b in range(STEP):
             t = first + b
-            conv = jnp.sum(u * power[b].reshape(shape), axis=0)
-            done[at(t), :] = gate[at(t), :] * (conv + base[at(t), :])
-        return u * power[STEP - 1].reshape(shape)
+            u = u * f
+            done[at(t), :] = gate[at(t), :] * (jnp.sum(u, axis=0) + base[at(t), :])
+        return u
 
     def emit(a):
         rows = pl.ds(pl.multiple_of(a * STEP, STEP), STEP)
@@ -453,7 +451,6 @@
             pltpu.VMEM((ROWS * SUBL, LANE), F32),
             pltpu.VMEM((ROWS * SUBL, LANE), F32),
             pltpu.VMEM((ROWS * SUBL, LANE), F32),
-            pltpu.VMEM((STEP, *flat), F32),
             pltpu.VMEM(flat, F32),
             pltpu.VMEM((2, *flat), F32),
             pltpu.VMEM((2, *flat), F32),

time: 31.6 us -> 31.1 us (0.984)
  Pallas kernels: 30.6 us -> 30.2 us
    pallas_call x1, Pallas kernels: 30.6 us -> 30.2 us  [shards(): pl.pallas_call(kernel, out_shape=pltpu.VMEM((ROWS, WIDTH), BF16), in_spec...]
where the time goes in v5:
time: 31.1 us; the launch traced here: 31 us
  Pallas kernels  30.2 us (97%)
  local copies, waits for them, and re-layouts  0.8 us (3%)
    pallas_call x1, Pallas kernels, shards(): pl.pallas_call(kernel, out_shape=pltpu.VMEM((ROWS, WIDTH), BF16), in_spec...  30.2 us
    unnamed x1, local copies, waits for them, and re-layouts  0.8 us

profile of v5, /device:TPU:96, one launch (start us, length us, event | category | flops | bytes accessed | tf_op | source)
XLA Modules:
  0.0 31.0 jit_solution(8846445124316637832)
XLA Ops:
  0.0 30.2 %hyena.1 = bf16[256,1024]{1,0:T(8,128)(2,1)S(1)} custom-call(bf16[256,1024]{1,0:T(8,128)(2,1)} %tokens.1, bf16[3,4096,1024]{2,1,0:T(8,128)(2,1)} %weight.1, f32[3,3,1024]{2,1,0:T(4,128)} %taps.1, f32[16,1024]{1,0:T(8,128)} %bitcast.3, f32[16,1024]{1,0:T(8,128)} %bitcast.4, f32[8,128]{1,0:T(8,128)} %bitcast.5), custom_call_target="tpu_custom_call" | custom-call | tf_op jit(solution)/shard_map/hyena/pallas_call | solution.py:440
  30.2 0.8 %copy.8 = bf16[256,1024]{1,0:T(8,128)(2,1)} copy(bf16[256,1024]{1,0:T(8,128)(2,1)S(1)} %hyena.1) | data formatting | bytes 1048576

commit v6 on v5

--- a/solution.py
+++ b/solution.py
@@ -28,7 +28,7 @@
 
 def kernel(
     tokens, weight, taps, residues, rates, skip, out,
-    w, x, acc, proj, src, base, gate, done, fac, fac_step, fac_part, res, rim_out, rim_in,
+    w, x, acc, proj, src, base, gate, done, fac, fac_step, fac_part, res, spread, rim_out, rim_in,
     taps_v, taps_t, rates_v, res_v, skip_v, state, row_sum, row_in, row_tot, grid_in, wpre, wtot,
     w_sem, tok_sem, par_sem, sib_s, sib_r, far_s, far_r, fwd_s, fwd_r, cross_s, cross_r,
     rim_s, rim_r, row_s, row_r, grid_s, grid_r, rim_ok, row_ok, grid_ok, seam_ok,
@@ -158,9 +158,10 @@
 
     for j in range(3):
         by_position(taps_t, j * 3 * SUBL, taps_v[j])
-    by_position(res, 0, res_v[...])
-    by_position(fac, 0, rates_v[...])
-    rate = fac[...]
+    by_position(spread, 0, res_v[...])
+    res[...] = spread[0:ORDER * SUBL, :]
+    by_position(spread, 0, rates_v[...])
+    rate = spread[0:ORDER * SUBL, :]
     for d in range(NY):
         below = (y + NY - d) % NY
         wtot[d] = jnp.exp(-rate * (ROWS * (NY - 1 - below)).astype(F32))
@@ -446,19 +447,20 @@
             pltpu.VMEM((4, 3, WIDTH, WIDTH), BF16),
             pltpu.VMEM((4, ROWS, WIDTH), BF16),
             pltpu.VMEM((3 * TILES, ROWS, TILE), F32),
-            pltpu.VMEM((3 * M * SUBL, LANE), F32),
+            pltpu.VMEM(((3 * M + 1) * SUBL, LANE), F32),
             pltpu.VMEM((ROWS * SUBL, LANE), F32),
             pltpu.VMEM((ROWS * SUBL, LANE), F32),
             pltpu.VMEM((ROWS * SUBL, LANE), F32),
-            pltpu.VMEM((ROWS * SUBL, LANE), F32),
+            pltpu.VMEM(((ROWS + 1) * SUBL, LANE), F32),
             pltpu.VMEM(flat, F32),
             pltpu.VMEM((2, *flat), F32),
             pltpu.VMEM((2, *flat), F32),
             pltpu.VMEM(flat, F32),
+            pltpu.VMEM(((ORDER + 1) * SUBL, LANE), F32),
             pltpu.VMEM((3 * 2 * SUBL, LANE), BF16),
             pltpu.VMEM((3 * 2 * SUBL, LANE), BF16),
             pltpu.VMEM((3, 3, WIDTH), F32),
-            pltpu.VMEM((9 * SUBL, LANE), F32),
+            pltpu.VMEM((10 * SUBL, LANE), F32),
             pltpu.VMEM((ORDER, WIDTH), F32),
             pltpu.VMEM((ORDER, WIDTH), F32),
             pltpu.VMEM((SUBL, LANE), F32),

time: 31.1 us -> 31.1 us (level)
  no operation moved by 1% of the time
where the time goes in v6:
time: 31.1 us; the launch traced here: 31 us
  Pallas kernels  30.2 us (97%)
  local copies, waits for them, and re-layouts  0.8 us (3%)
    pallas_call x1, Pallas kernels, shards(): pl.pallas_call(kernel, out_shape=pltpu.VMEM((ROWS, WIDTH), BF16), in_spec...  30.2 us
    unnamed x1, local copies, waits for them, and re-layouts  0.8 us

profile of v6, /device:TPU:96, one launch (start us, length us, event | category | flops | bytes accessed | tf_op | source)
XLA Modules:
  0.0 31.0 jit_solution(2046573387256367051)
XLA Ops:
  0.0 30.2 %hyena.1 = bf16[256,1024]{1,0:T(8,128)(2,1)S(1)} custom-call(bf16[256,1024]{1,0:T(8,128)(2,1)} %tokens.1, bf16[3,4096,1024]{2,1,0:T(8,128)(2,1)} %weight.1, f32[3,3,1024]{2,1,0:T(4,128)} %taps.1, f32[16,1024]{1,0:T(8,128)} %bitcast.3, f32[16,1024]{1,0:T(8,128)} %bitcast.4, f32[8,128]{1,0:T(8,128)} %bitcast.5), custom_call_target="tpu_custom_call" | custom-call | tf_op jit(solution)/shard_map/hyena/pallas_call | solution.py:441
  30.2 0.8 %copy.8 = bf16[256,1024]{1,0:T(8,128)(2,1)} copy(bf16[256,1024]{1,0:T(8,128)(2,1)S(1)} %hyena.1) | data formatting | bytes 1048576
